TPU v7x, 128 devices: a whole 4x4x4 slice. The times are simulated.
128 devices in a mesh: grp: 16 (over x, z), sub: 8 (over y, core).
Axes of the slice: x: 4, y: 4, z: 4, core: 2. Of those that a mesh axis runs over, the one named last changes fastest.
Arguments:
- tiles: float32 [32768, 64, 64], P(('grp', 'sub')), may hold values from -0.3 to 0.3
- owner: int32 [32768, 1], P(('grp', 'sub')), may hold values from 0 to 127; in each aligned block of 256 rows (0 to 255, 256 to 511, ...) at most 4 rows name the same one
- slot: int32 [32768], P(('grp', 'sub')), may hold values from 0 to 159
- nbr: int32 [4096, 5], P(('grp', 'sub')), may hold values from 0 to 4095, as said below
- shift: float32 [262144], P(('grp', 'sub')), may hold values from 1 to 10
- start: float32 [262144, 64], P(('grp', 'sub')), may hold values from -6 to 6
Outputs:
- basis: float32 [262144, 64], P(('grp', 'sub'))
- coarse: float32 [16, 64, 192], P('grp', 'sub')
Inputs may be any that keep to these rules, and one draw needn't show every extreme that they name: nbr[r,0] = r; the other entries of a row are distinct, differ from r, and lie among the block rows of devices r // 32 - 1, r // 32, r // 32 + 1 taken cyclically. Among the 256 tiles of one device, at most 4 name the same owner.
All inputs are finite; a program needn't handle non-finite values.
Results may differ from a plain program's by a relative error of at most 0.00015.
Values sent between devices are 32-bit elements; how exact they have to be, the bound alone decides.
A program may use at most 448 MiB of HBM per device.

v0:
```python
import jax
import jax.numpy as jnp
from jax import lax
from jax.sharding import PartitionSpec as P

K = 5
CAP = 4
ITERS = 2


def padded(cells, sides, width):
    for axis, dim in sides:
        count = lax.axis_size(axis)
        head = lax.slice_in_dim(cells, 0, width, axis=dim)
        tail = lax.slice_in_dim(cells, cells.shape[dim] - width, cells.shape[dim], axis=dim)
        cells = jnp.concatenate(
            [
                lax.ppermute(tail, axis, [(i, (i + 1) % count) for i in range(count)]),
                cells,
                lax.ppermute(head, axis, [((i + 1) % count, i) for i in range(count)]),
            ],
            axis=dim,
        )
    return cells


def shards(tiles, owner, slot, nbr, shift, start):
    devices = lax.axis_size(("grp", "sub"))
    my_index = lax.axis_index(("grp", "sub"))
    tile_size = tiles.shape[1]
    vectors = start.shape[1]
    blk_rows = nbr.shape[0]
    total_blocks = blk_rows * devices
    total_rows = total_blocks * tile_size
    dest = owner[:, 0]
    onehot = (dest[:, None] == jnp.arange(devices, dtype=jnp.int32)[None, :]).astype(jnp.int32)
    rank = jnp.sum(jnp.cumsum(onehot, axis=0) * onehot, axis=1) - 1
    position = dest * CAP + rank
    pad_slot = blk_rows * K
    send_tiles = (
        jnp.zeros((devices * CAP, tile_size, tile_size), jnp.float32).at[position].set(tiles)
    )
    send_slots = jnp.full((devices * CAP,), pad_slot, jnp.int32).at[position].set(slot)
    got_tiles, got_slots = (
        lax.all_to_all(
            send_tiles.reshape(devices, CAP, tile_size, tile_size),
            ("grp", "sub"),
            split_axis=0,
            concat_axis=0,
            tiled=True,
        ),
        lax.all_to_all(
            send_slots.reshape(devices, CAP),
            ("grp", "sub"),
            split_axis=0,
            concat_axis=0,
            tiled=True,
        ),
    )
    assembled = jax.ops.segment_sum(
        got_tiles.reshape(-1, tile_size, tile_size),
        got_slots.reshape(-1),
        num_segments=pad_slot + 1,
    )
    assembled = assembled[:pad_slot].reshape(blk_rows, K, tile_size, tile_size)
    eye = jnp.eye(tile_size, dtype=jnp.float32)
    assembled = assembled.at[:, 0].add(eye[None] * shift.reshape(blk_rows, tile_size)[:, None, :])
    local_index = (nbr - (my_index - 1) * blk_rows) % total_blocks

    def apply_op(basis):
        extended = padded(basis, ((("grp", "sub"), 0),), blk_rows * tile_size)
        blocks = extended.reshape(3 * blk_rows, tile_size, vectors)[local_index]
        return jnp.einsum("rkab,rkbc->rkac", assembled, blocks, precision=lax.Precision.HIGHEST)

    basis = start
    for step in range(ITERS):
        product = apply_op(basis).sum(axis=1).reshape(blk_rows * tile_size, vectors)
        local_gram = jnp.dot(product.T, product, precision=lax.Precision.HIGHEST)
        gram = lax.psum(local_gram, ("grp", "sub")) / total_rows
        factor = jnp.linalg.cholesky(gram)
        basis = lax.linalg.triangular_solve(
            factor, product, left_side=False, lower=True, transpose_a=True
        )
    mapped = apply_op(basis)
    inner = jnp.einsum(
        "rai,rkac->rkic",
        basis.reshape(blk_rows, tile_size, vectors),
        mapped,
        precision=lax.Precision.HIGHEST,
    )
    offset = (nbr // blk_rows - my_index + 1) % devices
    table = (offset[..., None] == jnp.arange(3, dtype=jnp.int32)).astype(jnp.float32)
    summed = jnp.einsum("rko,rkic->oic", table, inner, precision=lax.Precision.HIGHEST)
    members = lax.axis_size("sub")
    groups = lax.axis_size("grp")
    member = my_index % members
    first = (member == 0).astype(jnp.float32)
    last = (member == members - 1).astype(jnp.float32)
    lower = first * summed[0]
    middle = summed[1] + (1.0 - first) * summed[0] + (1.0 - last) * summed[2]
    upper = last * summed[2]
    term = jnp.concatenate([lower, middle, upper], axis=1) * (groups / total_rows)
    coarse = lax.psum_scatter(term[None], "sub", scatter_dimension=1, tiled=True)
    return (basis, coarse)


def solution(mesh):
    placed = (
        P(("grp", "sub"), None, None),
        P(("grp", "sub"), None),
        P(("grp", "sub")),
        P(("grp", "sub"), None),
        P(("grp", "sub")),
        P(("grp", "sub"), None),
    )
    return jax.shard_map(
        shards,
        mesh=mesh,
        in_specs=placed,
        out_specs=(P(("grp", "sub"), None), P("grp", "sub", None)),
        check_vma=False,
    )
```

profile of v0, /device:TPU:1, one launch (start us, length us, event | category | flops | bytes accessed | tf_op | source)
XLA Modules:
  0.0 613.2 jit_solution(12242759272756094441)
XLA Ops:
  5.6 11.5 %all-to-all-start = ((s32[128,1,4]{2,1,0:T(1,128)}), s32[128,1,4]{2,1,0:T(1,128)S(1)}, u32[]{:S(2)}, u32[]{:S(2)}) async-start(s32[128,1,4]{2,1,0:T(1,128)} %bitcast.7), calls=%async_computation | async-start | bytes 131072 | tf_op jit(solution)/shard_map/all_to_all | solution.py:52
  17.1 9.2 %copy.35 = f32[256,64,64]{2,1,0:T(8,128)} copy(f32[256,64,64]{0,2,1:T(8,128)} %param.11) | data formatting | bytes 8388608 | tf_op args[0]
  26.2 7.9 %broadcast_in_dim.11 = f32[512,64,64]{2,1,0:T(8,128)} broadcast(f32[]{:T(128)} %constant.128.clone.1), dimensions={} | broadcast | bytes 8388612 | tf_op jit(solution)/shard_map/broadcast_in_dim | solution.py:41
  34.1 37.2 %scatter_fusion = f32[512,64,64]{2,1,0:T(8,128)} fusion(f32[512,64,64]{2,1,0:T(8,128)} %broadcast_in_dim.11, s32[256]{0:T(256)S(1)} %bitcast.106, f32[256,64,64]{2,1,0:T(8,128)} %copy.35), kind=kCustom, calls=%fused_computation.4 | custom fusion | bytes 12583936 | tf_op jit(solution)/shard_map/scatter | solution.py:41
  71.3 17.9 %reshape.243 = f32[128,1,16384]{2,1,0:T(1,128)} reshape(f32[128,4,64,64]{3,2,1,0:T(8,128)} %bitcast.88) | data formatting | bytes 16777216
  89.2 10.3 %all-to-all-start.1 = ((f32[128,1,16384]{2,1,0:T(1,128)}), f32[128,1,16384]{2,1,0:T(1,128)}, u32[]{:S(2)}, u32[]{:S(2)}) async-start(f32[128,1,16384]{2,1,0:T(1,128)} %reshape.243), calls=%async_computation.1 | async-start | bytes 16777216 | tf_op jit(solution)/shard_map/all_to_all | solution.py:45
  103.4 93.6 %collective-permute-done = f32[2048,64]{0,1:T(8,128)S(1)} collective-permute-done((f32[2048,64]{0,1:T(8,128)S(1)}, f32[2048,64]{0,1:T(8,128)S(1)}, u32[]{:S(2)}, u32[]{:S(2)}) %collective-permute-start) | collective-permute-done | bytes 524320 | tf_op jit(solution)/shard_map/ppermute | solution.py:18
  197.0 2.8 collective-permute-done.1
  203.3 3.3 gather_fusion
  207.1 25.1 %reduce.10 = f32[128,16384]{1,0:T(8,128)} reduce(f32[128,1,16384]{2,1,0:T(1,128)} %all-to-all-done.1, f32[]{:T(128)} %broadcast.184), dimensions={1}, to_apply=%all_to_all.11.reduce_sub_computation | reduce | bytes 16777220 | tf_op jit(solution)/shard_map/all_to_all | solution.py:45
  232.2 13.1 %reshape.244 = f32[128,4,64,64]{3,2,1,0:T(8,128)} reshape(f32[128,16384]{1,0:T(8,128)} %reduce.10) | data formatting | bytes 16777216
  245.4 3.0 broadcast_in_dim.8
  248.3 77.0 %scatter_fusion.1 = f32[161,64,64]{2,1,0:T(8,128)} fusion(f32[161,64,64]{2,1,0:T(8,128)} %broadcast_in_dim.8, s32[512]{0:T(512)S(1)} %reshape.207, f32[512,64,64]{2,1,0:T(8,128)} %bitcast.90), kind=kCustom, calls=%fused_computation.5 | custom fusion | flops 2097152 | bytes 25167872 | tf_op jit(solution)/shard_map/scatter-add | solution.py:60
  325.3 2.9 slice.67
  328.5 8.6 %fusion.28 = f32[32,64,64,1]{2,1,3,0:T(8,128)S(1)} fusion(f32[32,5,64,64]{3,2,1,0:T(8,128)S(1)} %fusion, f32[32,5,64,64]{3,2,1,0:T(8,128)} %bitcast.94), kind=kOutput, calls=%fused_computation.80 | convolution fusion | flops 503316480 | bytes 5767168 | tf_op jit(solution)/shard_map/rkab,rkbc->rkac/dot_general | solution.py:73
  339.0 76.0 %psum.14 = f32[64,64]{0,1:T(8,128)S(1)} all-reduce(f32[64,64]{0,1:T(8,128)S(1)} %convolution_bitcast_fusion.5), channel_id=1, replica_groups=mesh['grp'=16,'sub'=8] {'grp','sub'}, use_global_device_ids=true, to_apply=%region_6.7 | all-reduce | flops 4096 | bytes 32768 | tf_op jit(solution)/shard_map/psum | solution.py:79
  415.1 5.8 cholesky.44
  422.3 4.9 custom-call.6
  429.8 5.3 collective-permute-done.2
  435.1 2.8 collective-permute-done.3
  441.3 3.3 gather_fusion.1
  444.5 8.7 %fusion.29 = f32[32,64,64,1]{2,1,3,0:T(8,128)S(1)} fusion(f32[32,5,64,64]{3,2,1,0:T(8,128)} %copy-done, f32[32,5,64,64]{3,2,1,0:T(8,128)} %bitcast.95), kind=kOutput, calls=%fused_computation.81 | convolution fusion | flops 503316480 | bytes 5767168 | tf_op jit(solution)/shard_map/rkab,rkbc->rkac/dot_general | solution.py:73
  455.1 72.5 %psum.15 = f32[64,64]{0,1:T(8,128)S(1)} all-reduce(f32[64,64]{0,1:T(8,128)S(1)} %convolution_bitcast_fusion.4), channel_id=1, replica_groups=mesh['grp'=16,'sub'=8] {'grp','sub'}, use_global_device_ids=true, to_apply=%region_9.12 | all-reduce | flops 4096 | bytes 32768 | tf_op jit(solution)/shard_map/psum | solution.py:79
  527.7 5.8 cholesky.55
  534.9 4.9 custom-call.7
  547.3 2.6 collective-permute-done.5
  553.3 3.3 gather_fusion.2
  556.5 11.6 %fusion.30 = f32[32,5,64,64]{2,3,1,0:T(8,128)S(1)} fusion(f32[32,5,64,64]{3,2,1,0:T(8,128)} %copy-done, f32[32,5,64,64]{3,2,1,0:T(8,128)} %bitcast.96), kind=kOutput, calls=%fused_computation.82 | convolution fusion | flops 503316480 | bytes 7864320 | tf_op jit(solution)/shard_map/rkab,rkbc->rkac/dot_general | solution.py:73
  568.2 6.4 %convolution_bitcast_fusion = f32[32,5,64,64]{2,3,1,0:T(8,128)} fusion(f32[32,5,64,64]{2,3,1,0:T(8,128)S(1)} %fusion.30, f32[32,64,64,1]{2,1,3,0:T(8,128)S(1)} %bitcast.99), kind=kOutput, calls=%fused_computation.6 | convolution fusion | flops 503316480 | bytes 5767168 | tf_op jit(solution)/shard_map/rai,rkac->rkic/dot_general | solution.py:85
  574.6 6.0 copy.48
  580.6 4.3 convolution_bitcast_fusion.3
  585.2 27.2 %all-reduce = f32[1,64,192]{2,0,1:T(1,128)S(1)} all-reduce(f32[1,64,192]{2,0,1:T(1,128)S(1)} %maximum_multiply_fusion), channel_id=2, replica_groups=mesh['grp'=16,'sub'=8] {'sub'}, use_global_device_ids=true, to_apply=%region_10.13.clone | all-reduce | flops 12288 | bytes 98304
  (75 shorter events, 36.7 us)
Async XLA Ops:
  5.6 83.6 %all-to-all-start = ((s32[128,1,4]{2,1,0:T(1,128)}), s32[128,1,4]{2,1,0:T(1,128)S(1)}, u32[]{:S(2)}, u32[]{:S(2)}) async-start(s32[128,1,4]{2,1,0:T(1,128)} %bitcast.7), calls=%async_computation | async-start | bytes 131072 | tf_op jit(solution)/shard_map/all_to_all | solution.py:52
  89.2 10.3 %copy-start.3 = (f32[2048,64]{0,1:T(8,128)S(1)}, f32[2048,64]{0,1:T(8,128)}, u32[]{:S(2)}) copy-start(f32[2048,64]{0,1:T(8,128)} %param.16) | copy-start | bytes 1572868
  89.2 12.5 %copy-start.5 = (s32[32,5]{0,1:T(8,128)S(1)}, s32[32,5]{0,1:T(8,128)}, u32[]{:S(2)}) copy-start(s32[32,5]{0,1:T(8,128)} %param.14) | copy-start | bytes 1924
  89.2 12.7 %copy-start.4 = (f32[2048]{0:T(1024)S(1)}, f32[2048]{0:T(1024)}, u32[]{:S(2)}) copy-start(f32[2048]{0:T(1024)} %param.15) | copy-start | bytes 24580
  89.2 117.3 %all-to-all-start.1 = ((f32[128,1,16384]{2,1,0:T(1,128)}), f32[128,1,16384]{2,1,0:T(1,128)}, u32[]{:S(2)}, u32[]{:S(2)}) async-start(f32[128,1,16384]{2,1,0:T(1,128)} %reshape.243), calls=%async_computation.1 | async-start | bytes 16777216 | tf_op jit(solution)/shard_map/all_to_all | solution.py:45
  99.5 97.5 %collective-permute-start = (f32[2048,64]{0,1:T(8,128)S(1)}, f32[2048,64]{0,1:T(8,128)S(1)}, u32[]{:S(2)}, u32[]{:S(2)}) collective-permute-start(f32[2048,64]{0,1:T(8,128)S(1)} %copy-done.3), channel_id=1, source_target_pairs={{0,1},{1,2},{2,3},{3,4},{4,5},{5,6},{6,7},{7,8},{8,9},{9,10},{10,1... | collective-permute-start | bytes 1572872 | tf_op jit(solution)/shard_map/ppermute | solution.py:18
  101.2 98.6 %collective-permute-start.1 = (f32[2048,64]{0,1:T(8,128)S(1)}, f32[2048,64]{0,1:T(8,128)S(1)}, u32[]{:S(2)}, u32[]{:S(2)}) collective-permute-start(f32[2048,64]{0,1:T(8,128)S(1)} %copy-done.3), channel_id=1, source_target_pairs={{1,0},{2,1},{3,2},{4,3},{5,4},{6,5},{7,6},{8,7},{9,8},{10,9},{11,1... | collective-permute-start | bytes 1572872 | tf_op jit(solution)/shard_map/ppermute | solution.py:20
  328.5 8.6 %copy-start = (f32[32,5,64,64]{3,2,1,0:T(8,128)}, f32[32,5,64,64]{3,2,1,0:T(8,128)S(1)}, u32[]{:S(2)}) copy-start(f32[32,5,64,64]{3,2,1,0:T(8,128)S(1)} %fusion) | copy-start | bytes 7864324
  428.5 6.6 %collective-permute-start.2 = (f32[2048,64]{0,1:T(8,128)S(1)}, f32[2048,64]{0,1:T(8,128)S(1)}, u32[]{:S(2)}, u32[]{:S(2)}) collective-permute-start(f32[2048,64]{0,1:T(8,128)S(1)} %convolution_bitcast_fusion.2), channel_id=1, source_target_pairs={{0,1},{1,2},{2,3},{3,4},{4,5},{5,6},{6,7},{7,8},{8,9},{9,10},{10,1... | collective-permute-start | bytes 1572872 | tf_op jit(solution)/shard_map/ppermute | solution.py:18
  429.0 8.9 %collective-permute-start.3 = (f32[2048,64]{0,1:T(8,128)S(1)}, f32[2048,64]{0,1:T(8,128)S(1)}, u32[]{:S(2)}, u32[]{:S(2)}) collective-permute-start(f32[2048,64]{0,1:T(8,128)S(1)} %convolution_bitcast_fusion.2), channel_id=1, source_target_pairs={{1,0},{2,1},{3,2},{4,3},{5,4},{6,5},{7,6},{8,7},{9,8},{10,9},{11,1... | collective-permute-start | bytes 1572872 | tf_op jit(solution)/shard_map/ppermute | solution.py:20
  444.5 97.9 %copy-start.6 = (u32[128]{0:T(128)S(1)}, u32[128]{0:T(128)}, u32[]{:S(2)}) copy-start(u32[128]{0:T(128)} %constant.154) | copy-start | bytes 1540
  541.1 8.8 %copy-start.1 = (f32[2048,64]{0,1:T(8,128)}, f32[2048,64]{0,1:T(8,128)S(1)}, u32[]{:S(2)}) copy-start(f32[2048,64]{0,1:T(8,128)S(1)} %convolution_bitcast_fusion.1) | copy-start | bytes 1572868
  541.1 6.2 %collective-permute-start.4 = (f32[2048,64]{0,1:T(8,128)S(1)}, f32[2048,64]{0,1:T(8,128)S(1)}, u32[]{:S(2)}, u32[]{:S(2)}) collective-permute-start(f32[2048,64]{0,1:T(8,128)S(1)} %convolution_bitcast_fusion.1), channel_id=1, source_target_pairs={{0,1},{1,2},{2,3},{3,4},{4,5},{5,6},{6,7},{7,8},{8,9},{9,10},{10,1... | collective-permute-start | bytes 1572872 | tf_op jit(solution)/shard_map/ppermute | solution.py:18
  541.2 8.7 %collective-permute-start.5 = (f32[2048,64]{0,1:T(8,128)S(1)}, f32[2048,64]{0,1:T(8,128)S(1)}, u32[]{:S(2)}, u32[]{:S(2)}) collective-permute-start(f32[2048,64]{0,1:T(8,128)S(1)} %convolution_bitcast_fusion.1), channel_id=1, source_target_pairs={{1,0},{2,1},{3,2},{4,3},{5,4},{6,5},{7,6},{8,7},{9,8},{10,9},{11,1... | collective-permute-start | bytes 1572872 | tf_op jit(solution)/shard_map/ppermute | solution.py:20
  556.5 11.7 %copy-start.2 = (f32[2048,64]{1,0:T(8,128)S(1)}, f32[2048,64]{1,0:T(8,128)}, u32[]{:S(2)}) copy-start(f32[2048,64]{1,0:T(8,128)} %copy.64) | copy-start | bytes 1572868
where the time goes:
time: 624 us; the launch traced here: 613 us
  blocking collectives  176 us (28%)
  other arithmetic  133 us (21%)
  local copies, waits for them, and re-layouts  120 us (19%)
  waiting for transfers between devices  109 us (17%)
  matrix products  45.9 us (7%)
  starting transfers between devices  26.5 us (4%)
    psum x2, blocking collectives, shards(): gram = lax.psum(local_gram, ('grp', 'sub')) / total_rows  148 us
    ppermute x3, waiting for transfers between devices, padded(): lax.ppermute(tail, axis, [(i, (i + 1) % count) for i in range(count)])  101 us
    scatter-add x1, other arithmetic, shards(): jax.ops.segment_sum(got_tiles.reshape(-1, tile_size, tile_size), got_slot...  77 us
    unnamed x21, local copies, waits for them, and re-layouts  41.4 us
    scatter x1, local copies, waits for them, and re-layouts, shards(): jnp.zeros((devices * CAP, tile_size, tile_size), jnp.float32).at[position]  37.2 us
    dot_general x3, matrix products, apply_op(): jnp.einsum('rkab,rkbc->rkac', assembled, blocks, precision=lax.Precision....  28.9 us
    unnamed x1, blocking collectives  27.2 us
    all_to_all x1, other arithmetic, shards(): lax.all_to_all(send_tiles.reshape(devices, CAP, tile_size, tile_size), ('...  25.1 us
  transfers between devices with their start and end apart: 8, of which 6 were waited for; matrix products, arithmetic and copies ran while one was open for 13% of the time, Pallas kernels for 0%

commit v1 on v0

v1 whole, which is shorter than its diff:
```python
import functools

import jax
import jax.numpy as jnp
from jax import lax
from jax.experimental import pallas as pl
from jax.experimental.pallas import tpu as pltpu
from jax.sharding import PartitionSpec as P

K = 5
CAP = 4
TS = 64
HALF = 32
LANES = 128
BLK = 32
ROWS = BLK * TS
PAIRS = ROWS // LANES
SLOTS = BLK * K
NT = (((1,), (1,)), ((), ()))
NN = (((1,), (0,)), ((), ()))
MESH = pl.DeviceIdType.MESH
F32 = jnp.float32
BF16 = jnp.bfloat16


def dot(a, b, dims):
    return lax.dot_general(a, b, dims, preferred_element_type=F32)


def roll(x):
    return pltpu.roll(x, TS, axis=1)


def low_lanes(shape):
    return lax.broadcasted_iota(jnp.int32, shape, 1) < TS


def split(x):
    hi = x.astype(BF16)
    lo = (x - hi.astype(F32)).astype(BF16)
    return jnp.concatenate([hi, lo], axis=0)


def fold(out):
    t = out[:TS] + out[TS:]
    return t + roll(t)


def spread(x):
    low = low_lanes(x.shape)
    r = roll(x)
    return jnp.where(low, x, r), jnp.where(low, r, x)


def pack(x):
    return jnp.where(low_lanes((HALF, LANES)), x[:HALF], x[HALF:])


def half_masks():
    low = low_lanes((1, LANES)).astype(F32)
    return low.astype(BF16), (1.0 - low).astype(BF16)


def blocks_of(stack_ref, lidx_ref, r):
    return [stack_ref[lidx_ref[r * K + k]] for k in range(K)]


def apply_row(stack_ref, lidx_ref, op_ref, r, masks):
    low, high = masks
    b = blocks_of(stack_ref, lidx_ref, r)
    left = jnp.concatenate([b[0] * low + b[1] * high, b[2] * low + b[3] * high, b[4]], axis=1)
    return fold(dot(left, op_ref[r], NT))


def route_kernel(place_ref, x_ref, out_ref, packed, sem):
    half = pl.program_id(0)
    for c in range(HALF):
        block = jnp.concatenate(
            [x_ref[0, pl.ds(c * TS, TS), :], x_ref[1, pl.ds(c * TS, TS), :]], axis=0
        )
        packed[pl.ds(c, LANES, stride=HALF), :] = block.T

    def send(t, carry):
        src = packed.at[pl.ds(pl.multiple_of(t * HALF, HALF), HALF)]
        at = pl.multiple_of(place_ref[half * LANES + t] * HALF, HALF)
        pltpu.make_async_copy(src, out_ref.at[pl.ds(at, HALF)], sem).start()
        return carry

    lax.fori_loop(0, LANES, send, 0, unroll=8)
    pltpu.make_async_copy(packed, out_ref.at[pl.ds(0, LANES * HALF)], sem).wait()


def route(place, x, cells):
    count = x.shape[2]
    return pl.pallas_call(
        route_kernel,
        out_shape=jax.ShapeDtypeStruct((cells * HALF, LANES), F32),
        grid_spec=pltpu.PrefetchScalarGridSpec(
            num_scalar_prefetch=1,
            grid=(count // LANES,),
            in_specs=[pl.BlockSpec((2, HALF * TS, LANES), lambda i, *_: (0, 0, i))],
            out_specs=pl.BlockSpec(memory_space=pl.ANY),
            scratch_shapes=[pltpu.VMEM((LANES * HALF, LANES), F32), pltpu.SemaphoreType.DMA],
        ),
        compiler_params=pltpu.CompilerParams(vmem_limit_bytes=24 << 20),
    )(place, x)


GROUP = 64


def assemble_kernel(
    slots_ref, lidx_ref, got_ref, shift_ref, left_ref, own_ref, right_ref,
    op_ref, x_ref, g_ref, total, stack, halves,
):
    step = pl.program_id(0)

    @pl.when(step == 0)
    def _():
        total[...] = jnp.zeros_like(total)

    def add(p, carry):
        at = pl.ds(pl.multiple_of(slots_ref[step * GROUP + p] * HALF, HALF), HALF)
        total[at] = total[at] + got_ref[pl.ds(pl.multiple_of(p * HALF, HALF), HALF)]
        return carry

    lax.fori_loop(0, GROUP, add, 0, unroll=4)

    @pl.when(step == pl.num_programs(0) - 1)
    def _():
        low = low_lanes((HALF, LANES))
        row = lax.broadcasted_iota(jnp.int32, (HALF, LANES), 0)
        lane = lax.broadcasted_iota(jnp.int32, (HALF, LANES), 1)
        on_diagonal = (lane % TS) == row + HALF * (lane // TS)

        def form(r, carry):
            t = [total[pl.ds(pl.multiple_of((r * K + k) * HALF, HALF), HALF)] for k in range(K)]
            t[0] = t[0] + jnp.where(on_diagonal, shift_ref[pl.ds(r, 1)], 0.0)
            for j in range(3):
                a = t[2 * j]
                b = t[2 * j + 1] if 2 * j + 1 < K else jnp.zeros_like(a)
                both = jnp.concatenate(
                    [jnp.where(low, a, roll(b)), jnp.where(low, roll(a), b)], axis=0
                )
                op_ref[r, :, pl.ds(j * LANES, LANES)] = split(both)
            return carry

        lax.fori_loop(0, BLK, form, 0, unroll=2)

        for part, ref in enumerate((left_ref, own_ref, right_ref)):
            def cut(q, carry, part=part, ref=ref):
                x = ref[:, pl.ds(pl.multiple_of(q * LANES, LANES), LANES)]
                even, odd = spread(x)
                stack[part * BLK + 2 * q] = split(even)
                stack[part * BLK + 2 * q + 1] = split(odd)
                return carry

            lax.fori_loop(0, PAIRS, cut, 0, unroll=2)

        masks = half_masks()

        def product(q, carry):
            even = apply_row(stack, lidx_ref, op_ref, 2 * q, masks)
            odd = apply_row(stack, lidx_ref, op_ref, 2 * q + 1, masks)
            x = jnp.where(low_lanes(even.shape), even, odd)
            at = pl.ds(pl.multiple_of(q * LANES, LANES), LANES)
            x_ref[:, at] = x
            halves[:, at] = split(x)
            return carry

        lax.fori_loop(0, PAIRS, product, 0, unroll=4)
        g_ref[...] = pack(fold(dot(halves[...], halves[...], NT)))


def assemble(slots, lidx, got, shift2, left, own, right):
    steps = slots.shape[0] // GROUP
    whole = lambda shape: pl.BlockSpec(shape, lambda i, *_: (0,) * len(shape))
    return pl.pallas_call(
        assemble_kernel,
        out_shape=(
            jax.ShapeDtypeStruct((BLK, 2 * TS, 3 * LANES), BF16),
            jax.ShapeDtypeStruct((TS, ROWS), F32),
            jax.ShapeDtypeStruct((HALF, LANES), F32),
        ),
        grid_spec=pltpu.PrefetchScalarGridSpec(
            num_scalar_prefetch=2,
            grid=(steps,),
            in_specs=[
                pl.BlockSpec((GROUP * HALF, LANES), lambda i, *_: (i, 0)),
                whole((BLK, LANES)),
                whole((TS, ROWS)),
                whole((TS, ROWS)),
                whole((TS, ROWS)),
            ],
            out_specs=(whole((BLK, 2 * TS, 3 * LANES)), whole((TS, ROWS)), whole((HALF, LANES))),
            scratch_shapes=[
                pltpu.VMEM(((SLOTS + 1) * HALF, LANES), F32),
                pltpu.VMEM((3 * BLK, 2 * TS, LANES), BF16),
                pltpu.VMEM((2 * TS, ROWS), BF16),
            ],
        ),
        compiler_params=pltpu.CompilerParams(vmem_limit_bytes=40 << 20),
    )(slots, lidx, got, shift2, left, own, right)


def inverse_factor(gram):
    lane = lax.broadcasted_iota(jnp.int32, (8, LANES), 1)
    row = lax.broadcasted_iota(jnp.int32, (8, LANES), 0)
    rolled = roll(gram)
    blocks = []
    for b in range(TS // 8):
        source = gram if b < 4 else rolled
        part = source[8 * (b % 4) : 8 * (b % 4) + 8]
        unit = (lane == row + (TS + 8 * b)).astype(F32)
        blocks.append(jnp.where(lane < TS, part, unit))
    pivots = [None] * (TS // 8)
    for j in range(TS):
        jb, js = j // 8, j % 8
        spreadcol = {
            b: jnp.broadcast_to(blocks[b][:, j : j + 1], (8, LANES)) for b in range(jb, TS // 8)
        }
        pivot = jnp.broadcast_to(spreadcol[jb][js : js + 1], (8, LANES))
        scaled = jnp.broadcast_to(blocks[jb][js : js + 1], (8, LANES)) * (1.0 / pivot)
        first = jnp.where(row == js, pivot, jnp.zeros_like(pivot))
        pivots[jb] = first if pivots[jb] is None else pivots[jb] + first
        for b in range(jb, TS // 8):
            col = spreadcol[b]
            if b == jb:
                col = jnp.where(row > js, col, 0.0)
            blocks[b] = blocks[b] - col * scaled
    a = jnp.concatenate([blk * lax.rsqrt(p) for blk, p in zip(blocks, pivots)], axis=0)
    return jnp.where(low_lanes(a.shape), roll(a), a)


def wide(inverse):
    hi = inverse.astype(BF16)
    lo = (inverse - hi.astype(F32)).astype(BF16)
    return jnp.concatenate([hi, lo], axis=1)


def times(inverse, x):
    return dot(inverse, jnp.concatenate([x, x], axis=0), NN)


def iterate_kernel(
    groups, members, total_rows,
    lidx_ref, op_ref, x1_ref, g1_ref,
    basis_ref, coarse_ref,
    stack, halo1, halo2, z, halves, mapped, sub_got, grp_got, partial, final, term, tail,
    halo_send, halo_recv, sub_send, sub_recv, grp_send, grp_recv, term_send, term_recv,
):
    g, s = lax.axis_index("grp"), lax.axis_index("sub")
    me = g * members + s
    count = groups * members
    after, before = lax.rem(me + 1, count), lax.rem(me + count - 1, count)

    def device(index):
        return (index // members, lax.rem(index, members))

    subs = [(g, lax.rem(s + i, members)) for i in range(1, members)]
    grps = [(lax.rem(g + i, groups), s) for i in range(1, groups)]

    barrier = pltpu.get_barrier_semaphore()
    for peer in [device(after), device(before)] + subs + grps:
        pl.semaphore_signal(barrier, inc=1, device_id=peer, device_id_type=MESH)
    pl.semaphore_wait(barrier, 2 + len(subs) + len(grps))

    def remote(src, dst, send, recv, peer):
        return pltpu.make_async_remote_copy(
            src_ref=src, dst_ref=dst, send_sem=send, recv_sem=recv,
            device_id=peer, device_id_type=MESH,
        )

    def send_halo(src, halo, n):
        copies = [
            remote(src, halo.at[0], halo_send.at[n, 0], halo_recv.at[n, 0], device(after)),
            remote(src, halo.at[1], halo_send.at[n, 1], halo_recv.at[n, 1], device(before)),
        ]
        for c in copies:
            c.start()
        return copies

    def send_sub(src, got, sends, recvs, n):
        copies = [
            remote(src, got.at[n, s], sends.at[n, i], recvs.at[n, i], peer)
            for i, peer in enumerate(subs)
        ]
        for c in copies:
            c.start()
        return copies

    def send_grp(src, n):
        copies = [
            remote(src, grp_got.at[n, g], grp_send.at[n, i], grp_recv.at[n, i], peer)
            for i, peer in enumerate(grps)
        ]
        for c in copies:
            c.start()
        return copies

    def take(copies):
        for c in copies:
            c.wait_recv()

    def sum_sub(n):
        acc = sub_got[n, 0]
        for i in range(1, members):
            acc = acc + sub_got[n, i]
        return acc

    def sum_grp(n):
        acc = grp_got[n, 0]
        for i in range(1, groups):
            acc = acc + grp_got[n, i]
        return acc

    def columns(q):
        return pl.ds(pl.multiple_of(q * LANES, LANES), LANES)

    def put_pair(base, q, x):
        even, odd = spread(x)
        stack[base + 2 * q] = split(even)
        stack[base + 2 * q + 1] = split(odd)

    started = []

    first = send_sub(g1_ref, sub_got, sub_send, sub_recv, 0)
    sub_got[0, s] = g1_ref[...]
    halo = send_halo(x1_ref, halo1, 0)

    def own1(q, carry):
        put_pair(BLK, q, x1_ref[:, columns(q)])
        return carry

    lax.fori_loop(0, PAIRS, own1, 0, unroll=2)
    take(first)
    partial[0] = sum_sub(0)
    grp_got[0, g] = partial[0]
    second = send_grp(partial.at[0], 0)
    take(halo)
    started += first + halo + second

    for side in range(2):
        def ext1(q, carry, side=side):
            put_pair(side * 2 * BLK, q, halo1[side, :, columns(q)])
            return carry

        lax.fori_loop(0, PAIRS, ext1, 0, unroll=2)

    masks = half_masks()

    def product(q, carry):
        even = apply_row(stack, lidx_ref, op_ref, 2 * q, masks)
        odd = apply_row(stack, lidx_ref, op_ref, 2 * q + 1, masks)
        z[:, columns(q)] = jnp.where(low_lanes(even.shape), even, odd)
        return carry

    lax.fori_loop(0, PAIRS, product, 0, unroll=4)
    halo = send_halo(z, halo2, 1)
    started += halo

    take(second)
    inverse1 = wide(inverse_factor(sum_grp(0) / total_rows))

    def own2(q, carry):
        x = times(inverse1, split(z[:, columns(q)]))
        halves[:, columns(q)] = split(x)
        put_pair(BLK, q, x)
        return carry

    lax.fori_loop(0, PAIRS, own2, 0, unroll=4)
    partial[1] = pack(fold(dot(halves[...], halves[...], NT)))
    first = send_sub(partial.at[1], sub_got, sub_send, sub_recv, 1)
    sub_got[1, s] = partial[1]

    take(halo)
    for side in range(2):
        def ext2(q, carry, side=side):
            x = times(inverse1, split(halo2[side, :, columns(q)]))
            put_pair(side * 2 * BLK, q, x)
            return carry

        lax.fori_loop(0, PAIRS, ext2, 0, unroll=4)

    take(first)
    partial[2] = sum_sub(1)
    grp_got[1, g] = partial[2]
    second = send_grp(partial.at[2], 1)
    started += first + second

    low, high = masks

    def project(q, carry):
        rows = []
        for r in (2 * q, 2 * q + 1):
            b = blocks_of(stack, lidx_ref, r)
            at = [lidx_ref[r * K + k] // BLK for k in range(K)]
            lefts = []
            for o in range(3):
                c = [(at[k] == o).astype(F32) for k in range(K)]
                m = [(low.astype(F32) * c[k] if k % 2 == 0 else high.astype(F32) * c[k]).astype(BF16) for k in range(K)]
                lefts.append(
                    jnp.concatenate([b[0] * m[0] + b[1] * m[1], b[2] * m[2] + b[3] * m[3], b[4] * m[4]], axis=1)
                )
            out = dot(jnp.concatenate(lefts, axis=0), op_ref[r], NT)
            rows.append([fold(out[o * 2 * TS : (o + 1) * 2 * TS]) for o in range(3)])
        for o in range(3):
            x = jnp.where(low_lanes((TS, LANES)), rows[0][o], rows[1][o])
            mapped[o, :, columns(q)] = split(x)
        return carry

    lax.fori_loop(0, PAIRS, project, 0, unroll=2)
    h = [fold(dot(halves[...], mapped[o], NT)) for o in range(3)]
    is_first = (s == 0).astype(F32)
    is_last = (s == members - 1).astype(F32)
    term[0:HALF] = pack(is_first * h[0])
    term[HALF : 2 * HALF] = pack(h[1] + (1.0 - is_first) * h[0] + (1.0 - is_last) * h[2])
    term[2 * HALF : 3 * HALF] = pack(is_last * h[2])
    terms = [
        remote(term, final.at[s], term_send.at[i], term_recv.at[i], peer)
        for i, peer in enumerate(subs)
    ]
    for c in terms:
        c.start()
    final[s] = term[...]
    started += terms

    take(second)
    inverse2 = inverse_factor(sum_grp(1) / total_rows)
    wide2 = wide(inverse2)

    def finish(q, carry):
        basis_ref[:, columns(q)] = times(wide2, halves[:, columns(q)])
        return carry

    lax.fori_loop(0, PAIRS, finish, 0, unroll=4)

    take(terms)
    acc = final[0]
    for i in range(1, members):
        acc = acc + final[i]
    square = inverse2[:, :TS]
    for o in range(3):
        packed = acc[o * HALF : (o + 1) * HALF]
        h = jnp.concatenate([packed[:, :TS], roll(packed)[:, :TS]], axis=0)
        left = lax.dot_general(square, h, NN, precision=lax.Precision.HIGHEST, preferred_element_type=F32)
        full = lax.dot_general(left, square, NT, precision=lax.Precision.HIGHEST, preferred_element_type=F32)
        tail[:, o * LANES : o * LANES + TS] = full * (groups / total_rows)
    mine = pl.ds(pl.multiple_of(s * 8, 8), 8)
    for o in range(3):
        coarse_ref[:, o * TS : (o + 1) * TS] = tail[mine, o * LANES : o * LANES + TS]
    for c in started:
        c.wait_send()


def iterate(lidx, op, x1, g1, groups, members, total_rows):
    vmem = pl.BlockSpec(memory_space=pltpu.VMEM)
    dma = pltpu.SemaphoreType.DMA
    return pl.pallas_call(
        functools.partial(iterate_kernel, groups, members, total_rows),
        out_shape=(
            jax.ShapeDtypeStruct((TS, ROWS), F32),
            jax.ShapeDtypeStruct((TS // members, 3 * TS), F32),
        ),
        in_specs=[pl.BlockSpec(memory_space=pltpu.SMEM), vmem, vmem, vmem],
        out_specs=(vmem, vmem),
        scratch_shapes=[
            pltpu.VMEM((3 * BLK, 2 * TS, LANES), BF16),
            pltpu.VMEM((2, TS, ROWS), F32),
            pltpu.VMEM((2, TS, ROWS), F32),
            pltpu.VMEM((TS, ROWS), F32),
            pltpu.VMEM((2 * TS, ROWS), BF16),
            pltpu.VMEM((3, 2 * TS, ROWS), BF16),
            pltpu.VMEM((2, members, HALF, LANES), F32),
            pltpu.VMEM((2, groups, HALF, LANES), F32),
            pltpu.VMEM((3, HALF, LANES), F32),
            pltpu.VMEM((members, 3 * HALF, LANES), F32),
            pltpu.VMEM((3 * HALF, LANES), F32),
            pltpu.VMEM((TS, 3 * LANES), F32),
            dma((2, 2)),
            dma((2, 2)),
            dma((2, members - 1)),
            dma((2, members - 1)),
            dma((2, groups - 1)),
            dma((2, groups - 1)),
            dma((members - 1,)),
            dma((members - 1,)),
        ],
        compiler_params=pltpu.CompilerParams(
            collective_id=1, has_side_effects=True, vmem_limit_bytes=48 << 20
        ),
    )(lidx, op, x1, g1)


def shards(tiles, owner, slot, nbr, shift, start):
    axes = ("grp", "sub")
    groups, members = lax.axis_size("grp"), lax.axis_size("sub")
    devices = groups * members
    me = lax.axis_index(axes)
    count = tiles.shape[0]
    total_blocks = BLK * devices
    dest = owner[:, 0]

    order = jnp.arange(count, dtype=jnp.int32)
    earlier = (dest[:, None] == dest[None, :]) & (order[:, None] < order[None, :])
    rank = jnp.sum(earlier.astype(jnp.int32), axis=0)
    place = dest * CAP + rank
    x = tiles.transpose(1, 2, 0).reshape(2, HALF * TS, count)
    sent = route(place, x, devices * CAP).reshape(devices, CAP * HALF, LANES)
    got = lax.all_to_all(sent, axes, split_axis=0, concat_axis=0, tiled=True)

    codes = lax.all_gather(dest * (SLOTS + 1) + slot, axes, axis=0, tiled=False)
    mine = codes // (SLOTS + 1) == me
    target = codes % (SLOTS + 1)
    upto = (order[:, None] <= order[None, :]).astype(BF16)
    seen = dot(mine.astype(BF16), upto, NN)
    slots = jnp.stack(
        [
            jnp.sum(jnp.where(mine & (seen == k + 1.0), target - SLOTS, 0), axis=1) + SLOTS
            for k in range(CAP)
        ],
        axis=1,
    ).reshape(devices * CAP)

    own = start.T
    forward = [(i, (i + 1) % devices) for i in range(devices)]
    backward = [((i + 1) % devices, i) for i in range(devices)]
    left = lax.ppermute(own, axes, forward)
    right = lax.ppermute(own, axes, backward)
    lidx = ((nbr - (me - 1) * BLK) % total_blocks).reshape(SLOTS)
    twice = jnp.tile(shift.reshape(BLK, TS), (1, 2))
    op, x1, g1 = assemble(slots, lidx, got.reshape(devices * CAP * HALF, LANES), twice, left, own, right)
    basis, coarse = iterate(lidx, op, x1, g1, groups, members, float(total_blocks * TS))
    return basis.T, coarse[None]


def solution(mesh):
    placed = (
        P(("grp", "sub"), None, None),
        P(("grp", "sub"), None),
        P(("grp", "sub")),
        P(("grp", "sub"), None),
        P(("grp", "sub")),
        P(("grp", "sub"), None),
    )
    return jax.shard_map(
        shards,
        mesh=mesh,
        in_specs=placed,
        out_specs=(P(("grp", "sub"), None), P("grp", "sub", None)),
        check_vma=False,
    )
```

time: 624 us -> 234 us (0.38); the launches traced: 613 us -> 233 us
  other arithmetic: 133 us -> 1.6 us
  local copies, waits for them, and re-layouts: 120 us -> 7.38 us
  waiting for transfers between devices: 109 us -> 0.01 us
  Pallas kernels: 0 us -> 73 us
  matrix products: 45.9 us -> 0.46 us
  blocking collectives: 176 us -> 136 us
  starting transfers between devices: 26.5 us -> 13.7 us
    psum x2 -> x0, blocking collectives: 148 us -> none  [shards(): gram = lax.psum(local_gram, ('grp', 'sub')) / total_rows]
    all_gather x0 -> x1, blocking collectives: none -> 136 us  [shards(): codes = lax.all_gather(dest * (SLOTS + 1) + slot, axes, axis=0, tiled=False)]
    ppermute x6 -> x2, waiting for transfers between devices: 109 us -> 0.01 us  [the longest x1 0.01 us: shards(): left = lax.ppermute(own, axes, forward)]
    scatter-add x2 -> x0, other arithmetic: 77.2 us -> none  [the longest x1 77 us: shards(): jax.ops.segment_sum(got_tiles.reshape(-1, tile_size, tile_size), got_slot...]
    pallas_call x0 -> x3, Pallas kernels: none -> 73 us  [the longest x1 48.4 us: iterate(): pl.pallas_call(functools.partial(iterate_kernel, groups, members, total_r...]
    dot_general x7 -> x1, matrix products: 43.3 us -> 0.46 us  [dot(): return lax.dot_general(a, b, dims, preferred_element_type=F32)]
    scatter x2 -> x0, local copies, waits for them, and re-layouts: 38.7 us -> none  [the longest x1 37.2 us: shards(): jnp.zeros((devices * CAP, tile_size, tile_size), jnp.float32).at[position]]
    unnamed x21 -> x12, local copies, waits for them, and re-layouts: 41.4 us -> 6.79 us
  transfers between devices with their start and end apart: 8 -> 3, of which waited for: 6 -> 0; matrix products, arithmetic and copies ran while one was open for 13% -> 0% of each run, Pallas kernels for 0% -> 0%
where the time goes in v1:
time: 234 us; the launch traced here: 233 us
  blocking collectives  136 us (58%)
  Pallas kernels  73 us (31%)
  starting transfers between devices  13.7 us (6%)
  local copies, waits for them, and re-layouts  7.38 us (3%)
    all_gather x1, blocking collectives, shards(): codes = lax.all_gather(dest * (SLOTS + 1) + slot, axes, axis=0, tiled=False)  136 us
    pallas_call x1, Pallas kernels, iterate(): pl.pallas_call(functools.partial(iterate_kernel, groups, members, total_r...  48.4 us
    pallas_call x1, Pallas kernels, assemble(): pl.pallas_call(assemble_kernel, out_shape=(jax.ShapeDtypeStruct((BLK, 2 *...  14 us
    all_to_all x1, starting transfers between devices, shards(): got = lax.all_to_all(sent, axes, split_axis=0, concat_axis=0, tiled=True)  12 us
    pallas_call x1, Pallas kernels, route(): pl.pallas_call(route_kernel, out_shape=jax.ShapeDtypeStruct((cells * HALF...  10.6 us
    unnamed x12, local copies, waits for them, and re-layouts  6.79 us
  transfers between devices with their start and end apart: 3, of which 0 were waited for; matrix products, arithmetic and copies ran while one was open for 0% of the time, Pallas kernels for 0%

profile of v1, /device:TPU:1, one launch (start us, length us, event | category | flops | bytes accessed | tf_op | source)
XLA Modules:
  0.0 233.2 jit_solution(14507604572260551912)
XLA Ops:
  0.6 0.9 convert_reduce_fusion
  1.5 0.7 multiply_add_fusion
  2.2 0.0 copy-start.1
  2.2 2.2 copy-done.1
  4.4 10.6 %shard_map.77 = f32[16384,128]{1,0:T(8,128)S(1)} custom-call(s32[256]{0:T(256)S(1)} %get-tuple-element.16.place_ref, f32[2,2048,256]{2,1,0:T(8,128)S(1)} %bitcast.59), custom_call_target="tpu_custom_call" | custom-call | tf_op jit(solution)/shard_map/pallas_call | solution.py:95
  15.0 0.0 copy-start
  15.1 3.2 %copy-done = f32[16384,128]{1,0:T(8,128)} copy-done((f32[16384,128]{1,0:T(8,128)}, f32[16384,128]{1,0:T(8,128)S(1)}, u32[]{:S(2)}) %copy-start) | copy-done | bytes 8388632
  18.3 0.0 copy-start.2
  18.3 0.0 copy-start.4
  18.3 0.0 copy-start.3
  18.3 12.0 %all-to-all-start = ((f32[128,128,128]{2,1,0:T(8,128)}), f32[128,128,128]{2,1,0:T(8,128)}, u32[]{:S(2)}, u32[]{:S(2)}) async-start(f32[128,128,128]{2,1,0:T(8,128)} %bitcast.58), calls=%async_computation | async-start | bytes 16777216 | tf_op jit(solution)/shard_map/all_to_all | solution.py:510
  30.2 0.0 copy-done.2
  30.2 1.7 collective-permute-start
  31.9 0.0 collective-permute-start.1
  31.9 136.3 %all-gather.1 = s32[128,1,256]{2,1,0:T(1,128)S(1)} all-gather(s32[1,1,256]{2,1,0:T(1,128)S(1)} %bitcast.67), channel_id=2, replica_groups=mesh['grp'=16,'sub'=8] {'grp','sub'}, dimensions={0}, use_global_device_ids=true | all-gather | bytes 132096 | tf_op jit(solution)/shard_map/all_gather | solution.py:512
  168.3 0.5 select_reduce_fusion.3
  168.8 0.1 copy.19
  168.9 0.1 reshape.61.slots_ref
  169.0 0.0 copy-done.4
  169.0 0.1 copy.15
  169.1 0.1 reshape.60.lidx_ref
  169.2 0.0 copy-done.3
  169.2 0.1 tile.10
  169.3 0.1 tile.12.shift_ref
  169.4 0.0 collective-permute-done.left_ref
  169.4 0.0 collective-permute-done.1.right_ref
  169.4 0.0 all-to-all-done
  169.4 14.0 %shard_map.78 = (bf16[32,128,384]{2,1,0:T(8,128)(2,1)S(1)}, f32[64,2048]{1,0:T(8,128)S(1)}, f32[32,128]{1,0:T(8,128)S(1)}) custom-call(s32[512]{0:T(512)S(1)} %reshape.61.slots_ref, s32[160]{0:T(256)S(1)} %reshape.60.lidx_ref, f32[16384,128]{1,0:T(8,128)} %bitcast.12.got_ref, f32[32,128]{1,0:T(8,128)S(1)} %tile.12.shift_ref, ...), custom_call_target="tpu_custom_call" | custom-call | tf_op jit(solution)/shard_map/pallas_call | solution.py:178
  183.4 48.4 %shard_map.79 = (f32[64,2048]{1,0:T(8,128)S(1)}, f32[8,192]{1,0:T(8,128)S(1)}) custom-call(s32[160]{0:T(256)S(1)} %reshape.60.lidx_ref, bf16[32,128,384]{2,1,0:T(8,128)(2,1)S(1)} %get-tuple-element.7.op_ref, f32[64,2048]{1,0:T(8,128)S(1)} %get-tuple-element.8.x1_ref, f32[32,128]{1,0:T(8,128)S(1)} %get-tuple-element.9.g1_ref), custom_call_target="tpu_custom_call" | custom-call | tf_op jit(solution)/shard_map/pallas_call | solution.py:459
  231.8 0.8 copy.44
  232.6 0.6 copy.45
  (5 shorter events, 0.0 us)
Async XLA Ops:
  2.2 2.2 copy-start.1
  15.0 3.2 %copy-start = (f32[16384,128]{1,0:T(8,128)}, f32[16384,128]{1,0:T(8,128)S(1)}, u32[]{:S(2)}) copy-start(f32[16384,128]{1,0:T(8,128)S(1)} %shard_map.77) | copy-start | bytes 25165828
  18.3 12.0 %copy-start.2 = (f32[2048,64]{0,1:T(8,128)S(1)}, f32[2048,64]{0,1:T(8,128)}, u32[]{:S(2)}) copy-start(f32[2048,64]{0,1:T(8,128)} %param.11) | copy-start | bytes 1572868
  18.3 150.7 %copy-start.4 = (s32[32,5]{0,1:T(8,128)S(1)}, s32[32,5]{0,1:T(8,128)}, u32[]{:S(2)}) copy-start(s32[32,5]{0,1:T(8,128)} %param.9) | copy-start | bytes 1924
  18.3 150.9 %copy-start.3 = (f32[2048]{0:T(1024)S(1)}, f32[2048]{0:T(1024)}, u32[]{:S(2)}) copy-start(f32[2048]{0:T(1024)} %param.10) | copy-start | bytes 24580
  18.3 151.1 %all-to-all-start = ((f32[128,128,128]{2,1,0:T(8,128)}), f32[128,128,128]{2,1,0:T(8,128)}, u32[]{:S(2)}, u32[]{:S(2)}) async-start(f32[128,128,128]{2,1,0:T(8,128)} %bitcast.58), calls=%async_computation | async-start | bytes 16777216 | tf_op jit(solution)/shard_map/all_to_all | solution.py:510
  30.2 139.2 %collective-permute-start = (f32[64,2048]{1,0:T(8,128)S(1)}, f32[64,2048]{1,0:T(8,128)S(1)}, u32[]{:S(2)}, u32[]{:S(2)}) collective-permute-start(f32[64,2048]{1,0:T(8,128)S(1)} %bitcast.60), channel_id=1, source_target_pairs={{0,1},{1,2},{2,3},{3,4},{4,5},{5,6},{6,7},{7,8},{8,9},{9,10},{10,1... | collective-permute-start | bytes 1572872 | tf_op jit(solution)/shard_map/ppermute | solution.py:528
  31.9 137.5 %collective-permute-start.1 = (f32[64,2048]{1,0:T(8,128)S(1)}, f32[64,2048]{1,0:T(8,128)S(1)}, u32[]{:S(2)}, u32[]{:S(2)}) collective-permute-start(f32[64,2048]{1,0:T(8,128)S(1)} %bitcast.61), channel_id=1, source_target_pairs={{1,0},{2,1},{3,2},{4,3},{5,4},{6,5},{7,6},{8,7},{9,8},{10,9},{11,1... | collective-permute-start | bytes 1572872 | tf_op jit(solution)/shard_map/ppermute | solution.py:529

commit v2 on v1

v2 whole, which is shorter than its diff:
```python
import functools

import jax
import jax.numpy as jnp
from jax import lax
from jax.experimental import pallas as pl
from jax.experimental.pallas import tpu as pltpu
from jax.sharding import PartitionSpec as P

K = 5
CAP = 4
TS = 64
HALF = 32
LANES = 128
BLK = 32
ROWS = BLK * TS
PAIRS = ROWS // LANES
SLOTS = BLK * K
NT = (((1,), (1,)), ((), ()))
NN = (((1,), (0,)), ((), ()))
STRIDE = 37
SHIFT = 51
MESH = pl.DeviceIdType.MESH
F32 = jnp.float32
BF16 = jnp.bfloat16


def dot(a, b, dims):
    return lax.dot_general(a, b, dims, preferred_element_type=F32)


def roll(x):
    return pltpu.roll(x, TS, axis=1)


def low_lanes(shape):
    return lax.broadcasted_iota(jnp.int32, shape, 1) < TS


def split(x):
    hi = x.astype(BF16)
    lo = (x - hi.astype(F32)).astype(BF16)
    return jnp.concatenate([hi, lo], axis=0)


def fold(out):
    t = out[:TS] + out[TS:]
    return t + roll(t)


def spread(x):
    low = low_lanes(x.shape)
    r = roll(x)
    return jnp.where(low, x, r), jnp.where(low, r, x)


def pack(x):
    return jnp.where(low_lanes((HALF, LANES)), x[:HALF], x[HALF:])


def half_masks():
    low = low_lanes((1, LANES)).astype(F32)
    return low.astype(BF16), (1.0 - low).astype(BF16)


def blocks_of(stack_ref, lidx_ref, r):
    return [stack_ref[lidx_ref[r * K + k]] for k in range(K)]


def apply_row(stack_ref, lidx_ref, op_ref, r, masks):
    low, high = masks
    b = blocks_of(stack_ref, lidx_ref, r)
    left = jnp.concatenate([b[0] * low + b[1] * high, b[2] * low + b[3] * high, b[4]], axis=1)
    return fold(dot(left, op_ref[r], NT))


def inverse_factor(gram):
    lane = lax.broadcasted_iota(jnp.int32, (8, LANES), 1)
    row = lax.broadcasted_iota(jnp.int32, (8, LANES), 0)
    rolled = roll(gram)
    blocks = []
    for b in range(TS // 8):
        source = gram if b < 4 else rolled
        part = source[8 * (b % 4) : 8 * (b % 4) + 8]
        unit = (lane == row + (TS + 8 * b)).astype(F32)
        blocks.append(jnp.where(lane < TS, part, unit))
    for jb in range(TS // 8):
        cols = {
            b: [
                jnp.broadcast_to(blocks[b][:, 8 * jb + m : 8 * jb + m + 1], (8, LANES))
                for m in range(8)
            ]
            for b in range(jb, TS // 8)
        }
        e = [[jnp.broadcast_to(cols[jb][m][i : i + 1], (8, LANES)) for m in range(i + 1)] for i in range(8)]
        rows = [jnp.broadcast_to(blocks[jb][i : i + 1], (8, LANES)) for i in range(8)]
        l = [[None] * 8 for _ in range(8)]
        inv = []
        for m in range(8):
            inv.append(1.0 / e[m][m])
            for i in range(m + 1, 8):
                l[i][m] = e[i][m] * inv[m]
            for i in range(m + 1, 8):
                for k in range(m + 1, i + 1):
                    e[i][k] = e[i][k] - l[i][m] * e[k][m]
                rows[i] = rows[i] - l[i][m] * rows[m]
        solved = [None] * 8
        for m in reversed(range(8)):
            acc = rows[m] * inv[m]
            for i in reversed(range(m + 1, 8)):
                acc = acc - l[i][m] * solved[i]
            solved[m] = acc
        for b in range(jb + 1, TS // 8):
            acc = [cols[b][m] * solved[m] for m in range(8)]
            while len(acc) > 1:
                acc = [acc[i] + acc[i + 1] for i in range(0, len(acc), 2)]
            blocks[b] = blocks[b] - acc[0]
        done = rows[0] * lax.rsqrt(e[0][0])
        for m in range(1, 8):
            done = jnp.where(row == m, rows[m] * lax.rsqrt(e[m][m]), done)
        blocks[jb] = done
    a = jnp.concatenate(blocks, axis=0)
    return jnp.where(low_lanes(a.shape), roll(a), a)


def wide(inverse):
    hi = inverse.astype(BF16)
    lo = (inverse - hi.astype(F32)).astype(BF16)
    return jnp.concatenate([hi, lo], axis=1)


def times(inverse, x):
    return dot(inverse, jnp.concatenate([x, x], axis=0), NN)


def whole_kernel(
    groups, members, total_rows,
    index_ref, lidx_ref, info_ref, shift_ref, start_ref, x_ref,
    basis_ref, coarse_ref,
    tiles, packed, sent, got, info_got, total, op, x1,
    stack, halo0, halo1, halo2, z, halves, mapped, sub_got, grp_got, partial, final, term, tail,
    load_sem, tile_send, tile_recv, info_send, info_recv,
    halo_send, halo_recv, sub_send, sub_recv, grp_send, grp_recv, term_send, term_recv,
):
    g, s = lax.axis_index("grp"), lax.axis_index("sub")
    me = g * members + s
    count = groups * members
    after, before = lax.rem(me + 1, count), lax.rem(me + count - 1, count)

    def device(index):
        return (index // members, lax.rem(index, members))

    def peer_of(i):
        other = jnp.bitwise_xor(me, lax.rem(i * STRIDE + me * SHIFT, count - 1) + 1)
        return other, device(other)

    loads = [
        pltpu.make_async_copy(
            x_ref.at[:, :, pl.ds(h * LANES, LANES)], tiles.at[:, :, pl.ds(h * LANES, LANES)], load_sem.at[h]
        )
        for h in range(2)
    ]
    for c in loads:
        c.start()

    barrier = pltpu.get_barrier_semaphore()

    def greet(i, carry):
        pl.semaphore_signal(barrier, inc=1, device_id=peer_of(i)[1], device_id_type=MESH)
        return carry

    lax.fori_loop(0, count - 1, greet, 0)

    subs = [(g, lax.rem(s + i, members)) for i in range(1, members)]
    grps = [(lax.rem(g + i, groups), s) for i in range(1, groups)]

    for h in range(2):
        loads[h].wait()
        for c in range(HALF):
            block = jnp.concatenate(
                [
                    tiles[0, pl.ds(c * TS, TS), pl.ds(h * LANES, LANES)],
                    tiles[1, pl.ds(c * TS, TS), pl.ds(h * LANES, LANES)],
                ],
                axis=0,
            )
            packed[pl.ds(h * LANES, LANES), c, :] = block.T

    def tile(position):
        return packed[index_ref[position]]

    pl.semaphore_wait(barrier, count - 1)

    def remote(src, dst, send, recv, peer):
        return pltpu.make_async_remote_copy(
            src_ref=src, dst_ref=dst, send_sem=send, recv_sem=recv,
            device_id=peer, device_id_type=MESH,
        )

    def send_halo(src, halo, n):
        copies = [
            remote(src, halo.at[0], halo_send.at[n, 0], halo_recv.at[n, 0], device(after)),
            remote(src, halo.at[1], halo_send.at[n, 1], halo_recv.at[n, 1], device(before)),
        ]
        for c in copies:
            c.start()
        return copies

    def send_sub(src, got, sends, recvs, n):
        copies = [
            remote(src, got.at[n, s], sends.at[n, i], recvs.at[n, i], peer)
            for i, peer in enumerate(subs)
        ]
        for c in copies:
            c.start()
        return copies

    def send_grp(src, n):
        copies = [
            remote(src, grp_got.at[n, g], grp_send.at[n, i], grp_recv.at[n, i], peer)
            for i, peer in enumerate(grps)
        ]
        for c in copies:
            c.start()
        return copies

    def take(copies):
        for c in copies:
            c.wait_recv()

    def sum_sub(n):
        acc = sub_got[n, 0]
        for i in range(1, members):
            acc = acc + sub_got[n, i]
        return acc

    def sum_grp(n):
        acc = grp_got[n, 0]
        for i in range(1, groups):
            acc = acc + grp_got[n, i]
        return acc

    def columns(q):
        return pl.ds(pl.multiple_of(q * LANES, LANES), LANES)

    def put_pair(base, q, x):
        even, odd = spread(x)
        stack[base + 2 * q] = split(even)
        stack[base + 2 * q + 1] = split(odd)

    started = send_halo(start_ref, halo0, 0)
    halo = started[:]

    def info_copy(i):
        other, place = peer_of(i)
        return remote(info_ref.at[other], info_got.at[me], info_send, info_recv, place)

    def send_info(i, carry):
        info_copy(i).start()
        return carry

    def send_tiles(k):
        def send(i, carry):
            other, place = peer_of(i)
            sent[k, other] = tile(other * CAP + k)
            remote(sent.at[k, other], got.at[k, me], tile_send.at[k], tile_recv.at[k], place).start()
            return carry

        lax.fori_loop(0, count - 1, send, 0)

    send_tiles(0)
    lax.fori_loop(0, count - 1, send_info, 0)
    for k in range(1, CAP):
        send_tiles(k)
    for k in range(CAP):
        got[k, me] = tile(me * CAP + k)
    info_got[me] = info_ref[me]

    def own0(q, carry):
        put_pair(BLK, q, start_ref[:, columns(q)])
        return carry

    lax.fori_loop(0, PAIRS, own0, 0, unroll=2)
    take(halo)

    def spread_halo(ref, side, q, carry):
        put_pair(side * 2 * BLK, q, ref[side, :, columns(q)])
        return carry

    for side in range(2):
        lax.fori_loop(0, PAIRS, functools.partial(spread_halo, halo0, side), 0, unroll=2)

    def bulk(ref, send, recv):
        part = ref.at[pl.ds(0, count - 1)]
        return remote(part, part, send, recv, device(after))

    bulk(info_got, info_send, info_recv).wait_recv()
    slots = info_got[:, 0, :].T
    slot_iota = lax.broadcasted_iota(jnp.int32, (SLOTS, count), 0).astype(F32)
    for k in range(CAP):
        hot = (slot_iota == slots[k : k + 1]).astype(F32).astype(BF16)
        hot = jnp.concatenate([hot, hot], axis=1)
        bulk(got.at[k], tile_send.at[k], tile_recv.at[k]).wait_recv()

        def add(c, carry, k=k, hot=hot):
            new = dot(hot, split(got[k, :, c, :]), NN)
            total[c] = new if k == 0 else total[c] + new
            return carry

        lax.fori_loop(0, HALF, add, 0, unroll=2)

    low = low_lanes((HALF, LANES))
    row = lax.broadcasted_iota(jnp.int32, (HALF, LANES), 0)
    lane = lax.broadcasted_iota(jnp.int32, (HALF, LANES), 1)
    on_diagonal = (lane % TS) == row + HALF * (lane // TS)

    def form(r, carry):
        t = [total[:, r * K + k, :] for k in range(K)]
        t[0] = t[0] + jnp.where(on_diagonal, shift_ref[pl.ds(r, 1)], 0.0)
        for j in range(3):
            a = t[2 * j]
            b = t[2 * j + 1] if 2 * j + 1 < K else jnp.zeros_like(a)
            both = jnp.concatenate([jnp.where(low, a, roll(b)), jnp.where(low, roll(a), b)], axis=0)
            op[r, :, pl.ds(j * LANES, LANES)] = split(both)
        return carry

    lax.fori_loop(0, BLK, form, 0, unroll=2)

    masks = half_masks()

    def product(out, q, carry):
        even = apply_row(stack, lidx_ref, op, 2 * q, masks)
        odd = apply_row(stack, lidx_ref, op, 2 * q + 1, masks)
        out[:, columns(q)] = jnp.where(low_lanes(even.shape), even, odd)
        return carry

    lax.fori_loop(0, PAIRS, functools.partial(product, x1), 0, unroll=4)
    halo = send_halo(x1, halo1, 1)

    def own1(q, carry):
        x = x1[:, columns(q)]
        halves[:, columns(q)] = split(x)
        put_pair(BLK, q, x)
        return carry

    lax.fori_loop(0, PAIRS, own1, 0, unroll=2)
    partial[3] = pack(fold(dot(halves[...], halves[...], NT)))

    first = send_sub(partial.at[3], sub_got, sub_send, sub_recv, 0)
    sub_got[0, s] = partial[3]
    take(first)
    partial[0] = sum_sub(0)
    grp_got[0, g] = partial[0]
    second = send_grp(partial.at[0], 0)
    take(halo)
    started += first + halo + second

    for side in range(2):
        def ext1(q, carry, side=side):
            put_pair(side * 2 * BLK, q, halo1[side, :, columns(q)])
            return carry

        lax.fori_loop(0, PAIRS, ext1, 0, unroll=2)

    lax.fori_loop(0, PAIRS, functools.partial(product, z), 0, unroll=4)
    halo = send_halo(z, halo2, 2)
    started += halo

    take(second)
    inverse1 = wide(inverse_factor(sum_grp(0) / total_rows))

    def own2(q, carry):
        x = times(inverse1, split(z[:, columns(q)]))
        halves[:, columns(q)] = split(x)
        put_pair(BLK, q, x)
        return carry

    lax.fori_loop(0, PAIRS, own2, 0, unroll=4)
    partial[1] = pack(fold(dot(halves[...], halves[...], NT)))
    first = send_sub(partial.at[1], sub_got, sub_send, sub_recv, 1)
    sub_got[1, s] = partial[1]

    take(halo)
    for side in range(2):
        def ext2(q, carry, side=side):
            x = times(inverse1, split(halo2[side, :, columns(q)]))
            put_pair(side * 2 * BLK, q, x)
            return carry

        lax.fori_loop(0, PAIRS, ext2, 0, unroll=4)

    take(first)
    partial[2] = sum_sub(1)
    grp_got[1, g] = partial[2]
    second = send_grp(partial.at[2], 1)
    started += first + second

    low, high = masks

    def project(q, carry):
        rows = []
        for r in (2 * q, 2 * q + 1):
            b = blocks_of(stack, lidx_ref, r)
            at = [lidx_ref[r * K + k] // BLK for k in range(K)]
            lefts = []
            for o in range(3):
                c = [(at[k] == o).astype(F32) for k in range(K)]
                m = [(low.astype(F32) * c[k] if k % 2 == 0 else high.astype(F32) * c[k]).astype(BF16) for k in range(K)]
                lefts.append(
                    jnp.concatenate([b[0] * m[0] + b[1] * m[1], b[2] * m[2] + b[3] * m[3], b[4] * m[4]], axis=1)
                )
            out = dot(jnp.concatenate(lefts, axis=0), op[r], NT)
            rows.append([fold(out[o * 2 * TS : (o + 1) * 2 * TS]) for o in range(3)])
        for o in range(3):
            x = jnp.where(low_lanes((TS, LANES)), rows[0][o], rows[1][o])
            mapped[o, :, columns(q)] = split(x)
        return carry

    lax.fori_loop(0, PAIRS, project, 0, unroll=2)
    h = [fold(dot(halves[...], mapped[o], NT)) for o in range(3)]
    is_first = (s == 0).astype(F32)
    is_last = (s == members - 1).astype(F32)
    term[0:HALF] = pack(is_first * h[0])
    term[HALF : 2 * HALF] = pack(h[1] + (1.0 - is_first) * h[0] + (1.0 - is_last) * h[2])
    term[2 * HALF : 3 * HALF] = pack(is_last * h[2])
    terms = [
        remote(term, final.at[s], term_send.at[i], term_recv.at[i], peer)
        for i, peer in enumerate(subs)
    ]
    for c in terms:
        c.start()
    final[s] = term[...]
    started += terms

    take(second)
    inverse2 = inverse_factor(sum_grp(1) / total_rows)
    wide2 = wide(inverse2)

    def finish(q, carry):
        basis_ref[:, columns(q)] = times(wide2, halves[:, columns(q)])
        return carry

    lax.fori_loop(0, PAIRS, finish, 0, unroll=4)

    take(terms)
    acc = final[0]
    for i in range(1, members):
        acc = acc + final[i]
    square = inverse2[:, :TS]
    for o in range(3):
        packed = acc[o * HALF : (o + 1) * HALF]
        h = jnp.concatenate([packed[:, :TS], roll(packed)[:, :TS]], axis=0)
        left = lax.dot_general(square, h, NN, precision=lax.Precision.HIGHEST, preferred_element_type=F32)
        full = lax.dot_general(left, square, NT, precision=lax.Precision.HIGHEST, preferred_element_type=F32)
        tail[:, o * LANES : o * LANES + TS] = full * (groups / total_rows)
    mine = pl.ds(pl.multiple_of(s * 8, 8), 8)
    for o in range(3):
        coarse_ref[:, o * TS : (o + 1) * TS] = tail[mine, o * LANES : o * LANES + TS]
    for c in started:
        c.wait_send()
    for c in [bulk(info_got, info_send, info_recv)] + [
        bulk(sent.at[k], tile_send.at[k], tile_recv.at[k]) for k in range(CAP)
    ]:
        c.wait_send()


def whole(index, lidx, info, shift2, start, x, groups, members, total_rows):
    vmem, smem = pl.BlockSpec(memory_space=pltpu.VMEM), pl.BlockSpec(memory_space=pltpu.SMEM)
    dma = pltpu.SemaphoreType.DMA
    count = groups * members
    tiles = x.shape[2]
    return pl.pallas_call(
        functools.partial(whole_kernel, groups, members, total_rows),
        out_shape=(
            jax.ShapeDtypeStruct((TS, ROWS), F32),
            jax.ShapeDtypeStruct((TS // members, 3 * TS), F32),
        ),
        in_specs=[smem, smem, vmem, vmem, vmem, pl.BlockSpec(memory_space=pl.ANY)],
        out_specs=(vmem, vmem),
        scratch_shapes=[
            pltpu.VMEM((2, HALF * TS, tiles), F32),
            pltpu.VMEM((tiles, HALF, LANES), F32),
            pltpu.VMEM((CAP, count, HALF, LANES), F32),
            pltpu.VMEM((CAP, count, HALF, LANES), F32),
            pltpu.VMEM((count, 1, LANES), F32),
            pltpu.VMEM((HALF, SLOTS, LANES), F32),
            pltpu.VMEM((BLK, 2 * TS, 3 * LANES), BF16),
            pltpu.VMEM((TS, ROWS), F32),
            pltpu.VMEM((3 * BLK, 2 * TS, LANES), BF16),
            pltpu.VMEM((2, TS, ROWS), F32),
            pltpu.VMEM((2, TS, ROWS), F32),
            pltpu.VMEM((2, TS, ROWS), F32),
            pltpu.VMEM((TS, ROWS), F32),
            pltpu.VMEM((2 * TS, ROWS), BF16),
            pltpu.VMEM((3, 2 * TS, ROWS), BF16),
            pltpu.VMEM((2, members, HALF, LANES), F32),
            pltpu.VMEM((2, groups, HALF, LANES), F32),
            pltpu.VMEM((4, HALF, LANES), F32),
            pltpu.VMEM((members, 3 * HALF, LANES), F32),
            pltpu.VMEM((3 * HALF, LANES), F32),
            pltpu.VMEM((TS, 3 * LANES), F32),
            dma((2,)),
            dma((CAP,)),
            dma((CAP,)),
            dma,
            dma,
            dma((3, 2)),
            dma((3, 2)),
            dma((2, members - 1)),
            dma((2, members - 1)),
            dma((2, groups - 1)),
            dma((2, groups - 1)),
            dma((members - 1,)),
            dma((members - 1,)),
        ],
        compiler_params=pltpu.CompilerParams(
            collective_id=1, has_side_effects=True, vmem_limit_bytes=60 << 20
        ),
    )(index, lidx, info, shift2, start, x)


def shards(tiles, owner, slot, nbr, shift, start):
    axes = ("grp", "sub")
    groups, members = lax.axis_size("grp"), lax.axis_size("sub")
    devices = groups * members
    me = lax.axis_index(axes)
    count = tiles.shape[0]
    total_blocks = BLK * devices
    dest = owner[:, 0]

    order = jnp.arange(count, dtype=jnp.int32)
    earlier = (dest[:, None] == dest[None, :]) & (order[:, None] < order[None, :])
    rank = jnp.sum(earlier.astype(jnp.int32), axis=0)
    place = dest * CAP + rank
    hit = place[:, None] == jnp.arange(devices * CAP, dtype=jnp.int32)[None, :]
    index = jnp.sum(jnp.where(hit, order[:, None], 0), axis=0)
    named = jnp.sum(jnp.where(hit, slot[:, None] - SLOTS, 0), axis=0) + SLOTS
    info = jnp.pad(
        named.astype(F32).reshape(devices, 1, CAP),
        ((0, 0), (0, 0), (0, LANES - CAP)),
    )
    x = tiles.transpose(1, 2, 0).reshape(2, HALF * TS, count)
    lidx = ((nbr - (me - 1) * BLK) % total_blocks).reshape(SLOTS)
    twice = jnp.tile(shift.reshape(BLK, TS), (1, 2))
    basis, coarse = whole(
        index, lidx, info, twice, start.T, x, groups, members, float(total_blocks * TS)
    )
    return basis.T, coarse[None]


def solution(mesh):
    placed = (
        P(("grp", "sub"), None, None),
        P(("grp", "sub"), None),
        P(("grp", "sub")),
        P(("grp", "sub"), None),
        P(("grp", "sub")),
        P(("grp", "sub"), None),
    )
    return jax.shard_map(
        shards,
        mesh=mesh,
        in_specs=placed,
        out_specs=(P(("grp", "sub"), None), P("grp", "sub", None)),
        check_vma=False,
    )
```

time: 234 us -> 199 us (0.85)
  blocking collectives: 136 us -> 0 us
  Pallas kernels: 73 us -> 188 us
  starting transfers between devices: 13.7 us -> 0 us
    all_gather x1 -> x0, blocking collectives: 136 us -> none  [shards(): codes = lax.all_gather(dest * (SLOTS + 1) + slot, axes, axis=0, tiled=False)]
    pallas_call x3 -> x1, Pallas kernels: 73 us -> 188 us  [whole(): pl.pallas_call(functools.partial(whole_kernel, groups, members, total_row...]
    all_to_all x1 -> x0, starting transfers between devices: 12 us -> none  [shards(): got = lax.all_to_all(sent, axes, split_axis=0, concat_axis=0, tiled=True)]
    unnamed x12 -> x2, local copies, waits for them, and re-layouts: 6.79 us -> 3.17 us
  transfers between devices with their start and end apart: 3 -> 0, of which waited for: 0 -> 0; matrix products, arithmetic and copies ran while one was open for 0% -> 0% of each run, Pallas kernels for 0% -> 0%
where the time goes in v2:
time: 199 us
  Pallas kernels  188 us (94%)
  local copies, waits for them, and re-layouts  6.19 us (3%)
  other arithmetic  3.68 us (2%)
    pallas_call x1, Pallas kernels, whole(): pl.pallas_call(functools.partial(whole_kernel, groups, members, total_row...  188 us

profile of v2, /device:TPU:1, one launch (start us, length us, event | category | flops | bytes accessed | tf_op | source)
XLA Modules:
  0.0 198.5 jit_solution(18386092151232209555)
XLA Ops:
  0.6 0.7 broadcast_add_fusion
  1.3 0.9 convert_reduce_fusion
  2.2 0.7 multiply_add_fusion
  2.9 0.7 select_reduce_fusion
  3.6 0.7 add_select_fusion
  4.3 0.1 copy.10
  4.4 0.7 reshape.35.lidx_ref
  5.1 0.8 tile.10
  5.9 0.7 tile.12.shift_ref
  6.6 0.1 convert_element_type.20
  6.7 0.7 pad.4.info_ref
  7.4 188.0 %shard_map.77 = (f32[64,2048]{1,0:T(8,128)}, f32[8,192]{1,0:T(8,128)}) custom-call(s32[512]{0:T(512)} %get-tuple-element.7.index_ref, s32[160]{0:T(256)} %reshape.35.lidx_ref, f32[128,1,128]{2,1,0:T(1,128)} %pad.4.info_ref, f32[32,128]{1,0:T(8,128)} %tile.12.shift_ref, f32[64,2048]{1,0:T(8,128)} %bitcast.11, f32[2,2048,256]{2,1,0:T(8,128)} %bitcast.10), custom_call_target="tpu_custom_call" | custom-call | tf_op jit(solution)/shard_map/pallas_call | solution.py:472
  195.3 1.9 copy.14
  197.2 1.3 copy.15
  (2 shorter events, 0.0 us)

commit v3 on v2

--- a/solution.py
+++ b/solution.py
@@ -18,6 +18,7 @@
 SLOTS = BLK * K
 NT = (((1,), (1,)), ((), ()))
 NN = (((1,), (0,)), ((), ()))
+PIECES = 4
 STRIDE = 37
 SHIFT = 51
 MESH = pl.DeviceIdType.MESH
@@ -64,7 +65,7 @@
 
 
 def blocks_of(stack_ref, lidx_ref, r):
-    return [stack_ref[lidx_ref[r * K + k]] for k in range(K)]
+    return [stack_ref[jnp.clip(lidx_ref[k, r], 0, 3 * BLK - 1)] for k in range(K)]
 
 
 def apply_row(stack_ref, lidx_ref, op_ref, r, masks):
@@ -135,11 +136,11 @@
 
 def whole_kernel(
     groups, members, total_rows,
-    index_ref, lidx_ref, info_ref, shift_ref, start_ref, x_ref,
-    basis_ref, coarse_ref,
-    tiles, packed, sent, got, info_got, total, op, x1,
-    stack, halo0, halo1, halo2, z, halves, mapped, sub_got, grp_got, partial, final, term, tail,
-    load_sem, tile_send, tile_recv, info_send, info_recv,
+    owner_ref, slot_ref, nbr_ref, shift_ref, start_ref, x_ref,
+    halves, inverse_ref, acc_ref,
+    index_v, index_ref, lidx_v, lidx_ref, info_ref, tiles, packed, sent, got, info_got, total, op, x1,
+    stack, halo0, halo1, halo2, z, mapped, sub_got, grp_got, partial, final, term,
+    load_sem, table_sem, tile_send, tile_recv, info_send, info_recv,
     halo_send, halo_recv, sub_send, sub_recv, grp_send, grp_recv, term_send, term_recv,
 ):
     g, s = lax.axis_index("grp"), lax.axis_index("sub")
@@ -170,6 +171,40 @@
         return carry
 
     lax.fori_loop(0, count - 1, greet, 0)
+
+    amount = owner_ref.shape[1]
+    places = CAP * count
+
+    def column(x, width):
+        tall = jnp.broadcast_to(x, (8, x.shape[1])).T
+        return jnp.broadcast_to(tall[:, :1], (x.shape[1], width))
+
+    dest = owner_ref[...].astype(F32)
+    down = lax.broadcasted_iota(jnp.int32, (amount, amount), 0)
+    across = lax.broadcasted_iota(jnp.int32, (amount, amount), 1)
+    earlier = (column(dest, amount) == dest) & (down < across)
+    rank = jnp.sum(jnp.where(earlier, 1.0, 0.0), axis=0, keepdims=True)
+    place = column(rank * count + dest, places)
+    hit = place == lax.broadcasted_iota(jnp.int32, (amount, places), 1).astype(F32)
+    order = lax.broadcasted_iota(jnp.int32, (amount, places), 0).astype(F32)
+    index_v[...] = jnp.sum(jnp.where(hit, order, 0.0), axis=0, keepdims=True).astype(jnp.int32)
+    target = column(slot_ref[...].astype(F32) - SLOTS, places)
+    named = jnp.sum(jnp.where(hit, target, 0.0), axis=0, keepdims=True) + SLOTS
+    info = jnp.concatenate(
+        [named[:, k * count : (k + 1) * count] for k in range(CAP)] + [jnp.zeros((8 - CAP, count), F32)],
+        axis=0,
+    )
+    info_ref[:, 0, :] = jnp.concatenate([info.T, jnp.zeros((count, LANES - 8), F32)], axis=1)
+    near = nbr_ref[...] - (me - 1) * BLK
+    near = jnp.where(near < 0, near + BLK * count, near)
+    near = jnp.where(near >= BLK * count, near - BLK * count, near)
+    lidx_v[0:K, 0:BLK] = jnp.minimum(near, 3 * BLK - 1)
+    tables = [
+        pltpu.make_async_copy(index_v, index_ref, table_sem.at[0]),
+        pltpu.make_async_copy(lidx_v, lidx_ref, table_sem.at[1]),
+    ]
+    for c in tables:
+        c.start()
 
     subs = [(g, lax.rem(s + i, members)) for i in range(1, members)]
     grps = [(lax.rem(g + i, groups), s) for i in range(1, groups)]
@@ -187,8 +222,10 @@
             packed[pl.ds(h * LANES, LANES), c, :] = block.T
 
     def tile(position):
-        return packed[index_ref[position]]
-
+        return packed[jnp.clip(index_ref[0, position], 0, amount - 1)]
+
+    for c in tables:
+        c.wait()
     pl.semaphore_wait(barrier, count - 1)
 
     def remote(src, dst, send, recv, peer):
@@ -197,10 +234,19 @@
             device_id=peer, device_id_type=MESH,
         )
 
-    def send_halo(src, halo, n):
+    def piece(p):
+        return pl.ds(p * (ROWS // PIECES), ROWS // PIECES)
+
+    def send_halo(src, halo, n, p):
         copies = [
-            remote(src, halo.at[0], halo_send.at[n, 0], halo_recv.at[n, 0], device(after)),
-            remote(src, halo.at[1], halo_send.at[n, 1], halo_recv.at[n, 1], device(before)),
+            remote(
+                src.at[:, piece(p)], halo.at[0, :, piece(p)],
+                halo_send.at[n, 0, p], halo_recv.at[n, 0, p], device(after),
+            ),
+            remote(
+                src.at[:, piece(p)], halo.at[1, :, piece(p)],
+                halo_send.at[n, 1, p], halo_recv.at[n, 1, p], device(before),
+            ),
         ]
         for c in copies:
             c.start()
@@ -248,8 +294,6 @@
         stack[base + 2 * q] = split(even)
         stack[base + 2 * q + 1] = split(odd)
 
-    started = send_halo(start_ref, halo0, 0)
-    halo = started[:]
 
     def info_copy(i):
         other, place = peer_of(i)
@@ -259,72 +303,115 @@
         info_copy(i).start()
         return carry
 
+    def send_tile(k, i):
+        other, place = peer_of(i)
+        sent[k, other] = tile(k * count + other)
+        remote(sent.at[k, other], got.at[k, me], tile_send.at[k], tile_recv.at[k], place).start()
+
     def send_tiles(k):
         def send(i, carry):
-            other, place = peer_of(i)
-            sent[k, other] = tile(other * CAP + k)
-            remote(sent.at[k, other], got.at[k, me], tile_send.at[k], tile_recv.at[k], place).start()
+            send_tile(k, i)
             return carry
 
         lax.fori_loop(0, count - 1, send, 0)
-
-    send_tiles(0)
-    lax.fori_loop(0, count - 1, send_info, 0)
-    for k in range(1, CAP):
-        send_tiles(k)
-    for k in range(CAP):
-        got[k, me] = tile(me * CAP + k)
-    info_got[me] = info_ref[me]
-
-    def own0(q, carry):
-        put_pair(BLK, q, start_ref[:, columns(q)])
-        return carry
-
-    lax.fori_loop(0, PAIRS, own0, 0, unroll=2)
-    take(halo)
-
-    def spread_halo(ref, side, q, carry):
-        put_pair(side * 2 * BLK, q, ref[side, :, columns(q)])
-        return carry
-
-    for side in range(2):
-        lax.fori_loop(0, PAIRS, functools.partial(spread_halo, halo0, side), 0, unroll=2)
 
     def bulk(ref, send, recv):
         part = ref.at[pl.ds(0, count - 1)]
         return remote(part, part, send, recv, device(after))
 
+    def arrived(k):
+        bulk(got.at[k], tile_send.at[k], tile_recv.at[k]).wait_recv()
+
+    for k in range(CAP):
+        got[k, me] = tile(k * count + me)
+    info_got[me] = info_ref[me]
+    send_tiles(0)
+    lax.fori_loop(0, count - 1, send_info, 0)
+    send_tiles(1)
+
+    def own0(q, carry):
+        put_pair(BLK, q, start_ref[:, columns(q)])
+        return carry
+
+    lax.fori_loop(0, PAIRS, own0, 0, unroll=2)
+
     bulk(info_got, info_send, info_recv).wait_recv()
     slots = info_got[:, 0, :].T
     slot_iota = lax.broadcasted_iota(jnp.int32, (SLOTS, count), 0).astype(F32)
-    for k in range(CAP):
+
+    def hot_of(k):
         hot = (slot_iota == slots[k : k + 1]).astype(F32).astype(BF16)
-        hot = jnp.concatenate([hot, hot], axis=1)
-        bulk(got.at[k], tile_send.at[k], tile_recv.at[k]).wait_recv()
-
-        def add(c, carry, k=k, hot=hot):
-            new = dot(hot, split(got[k, :, c, :]), NN)
-            total[c] = new if k == 0 else total[c] + new
+        return jnp.concatenate([hot, hot], axis=1)
+
+    def add(k, hot, c):
+        new = dot(hot, split(got[k, :, c, :]), NN)
+        total[c] = new if k == 0 else total[c] + new
+
+    for k in range(2, CAP):
+        arrived(k - 2)
+        hot = hot_of(k - 2)
+
+        def both(c, carry, k=k, hot=hot):
+            for j in range(count // HALF):
+                i = c * (count // HALF) + j
+                if j < count // HALF - 1:
+                    send_tile(k, i)
+                else:
+                    @pl.when(i < count - 1)
+                    def _():
+                        send_tile(k, i)
+            add(k - 2, hot, c)
             return carry
 
-        lax.fori_loop(0, HALF, add, 0, unroll=2)
+        lax.fori_loop(0, HALF, both, 0)
+
+    halo = [send_halo(start_ref, halo0, 0, p) for p in range(PIECES)]
+    started = sum(halo, [])
+    for k in range(CAP - 2, CAP):
+        arrived(k)
+        hot = hot_of(k)
+
+        def one(c, carry, k=k, hot=hot):
+            add(k, hot, c)
+            return carry
+
+        lax.fori_loop(0, HALF, one, 0, unroll=8)
 
     low = low_lanes((HALF, LANES))
     row = lax.broadcasted_iota(jnp.int32, (HALF, LANES), 0)
     lane = lax.broadcasted_iota(jnp.int32, (HALF, LANES), 1)
     on_diagonal = (lane % TS) == row + HALF * (lane // TS)
 
-    def form(r, carry):
-        t = [total[:, r * K + k, :] for k in range(K)]
-        t[0] = t[0] + jnp.where(on_diagonal, shift_ref[pl.ds(r, 1)], 0.0)
-        for j in range(3):
-            a = t[2 * j]
-            b = t[2 * j + 1] if 2 * j + 1 < K else jnp.zeros_like(a)
-            both = jnp.concatenate([jnp.where(low, a, roll(b)), jnp.where(low, roll(a), b)], axis=0)
-            op[r, :, pl.ds(j * LANES, LANES)] = split(both)
-        return carry
-
-    lax.fori_loop(0, BLK, form, 0, unroll=2)
+    def form(q, carry):
+        both = shift_ref[pl.ds(q, 1)]
+        shift_of = [jnp.where(low[:1], both, roll(both)), jnp.where(low[:1], roll(both), both)]
+        for b in range(2):
+            r = 2 * q + b
+            t = [total[:, r * K + k, :] for k in range(K)]
+            t[0] = t[0] + jnp.where(on_diagonal, shift_of[b], 0.0)
+            for j in range(3):
+                x = t[2 * j]
+                y = t[2 * j + 1] if 2 * j + 1 < K else jnp.zeros_like(x)
+                pair = jnp.concatenate([jnp.where(low, x, roll(y)), jnp.where(low, roll(x), y)], axis=0)
+                op[r, :, pl.ds(j * LANES, LANES)] = split(pair)
+        return carry
+
+    lax.fori_loop(0, PAIRS, form, 0, unroll=2)
+
+    def spread_halo(ref, side, q, carry):
+        put_pair(side * 2 * BLK, q, ref[side, :, columns(q)])
+        return carry
+
+    def spread_halos(ref, halo):
+        for p in range(PIECES):
+            take(halo[p])
+            for side in range(2):
+                lax.fori_loop(
+                    p * (PAIRS // PIECES), (p + 1) * (PAIRS // PIECES),
+                    functools.partial(spread_halo, ref, side), 0, unroll=4,
+                )
+
+    spread_halos(halo0, halo)
 
     masks = half_masks()
 
@@ -334,8 +421,18 @@
         out[:, columns(q)] = jnp.where(low_lanes(even.shape), even, odd)
         return carry
 
-    lax.fori_loop(0, PAIRS, functools.partial(product, x1), 0, unroll=4)
-    halo = send_halo(x1, halo1, 1)
+    def products(out, halo, n):
+        copies = []
+        for p in range(PIECES):
+            lax.fori_loop(
+                p * (PAIRS // PIECES), (p + 1) * (PAIRS // PIECES),
+                functools.partial(product, out), 0, unroll=4,
+            )
+            copies.append(send_halo(out, halo, n, p))
+        return copies
+
+    halo = products(x1, halo1, 1)
+    started += sum(halo, [])
 
     def own1(q, carry):
         x = x1[:, columns(q)]
@@ -352,19 +449,10 @@
     partial[0] = sum_sub(0)
     grp_got[0, g] = partial[0]
     second = send_grp(partial.at[0], 0)
-    take(halo)
-    started += first + halo + second
-
-    for side in range(2):
-        def ext1(q, carry, side=side):
-            put_pair(side * 2 * BLK, q, halo1[side, :, columns(q)])
-            return carry
-
-        lax.fori_loop(0, PAIRS, ext1, 0, unroll=2)
-
-    lax.fori_loop(0, PAIRS, functools.partial(product, z), 0, unroll=4)
-    halo = send_halo(z, halo2, 2)
-    started += halo
+    started += first + second
+    spread_halos(halo1, halo)
+    halo = products(z, halo2, 2)
+    started += sum(halo, [])
 
     take(second)
     inverse1 = wide(inverse_factor(sum_grp(0) / total_rows))
@@ -380,14 +468,17 @@
     first = send_sub(partial.at[1], sub_got, sub_send, sub_recv, 1)
     sub_got[1, s] = partial[1]
 
-    take(halo)
-    for side in range(2):
-        def ext2(q, carry, side=side):
-            x = times(inverse1, split(halo2[side, :, columns(q)]))
-            put_pair(side * 2 * BLK, q, x)
-            return carry
-
-        lax.fori_loop(0, PAIRS, ext2, 0, unroll=4)
+    def ext2(side, q, carry):
+        put_pair(side * 2 * BLK, q, times(inverse1, split(halo2[side, :, columns(q)])))
+        return carry
+
+    for p in range(PIECES):
+        take(halo[p])
+        for side in range(2):
+            lax.fori_loop(
+                p * (PAIRS // PIECES), (p + 1) * (PAIRS // PIECES),
+                functools.partial(ext2, side), 0, unroll=4,
+            )
 
     take(first)
     partial[2] = sum_sub(1)
@@ -401,7 +492,7 @@
         rows = []
         for r in (2 * q, 2 * q + 1):
             b = blocks_of(stack, lidx_ref, r)
-            at = [lidx_ref[r * K + k] // BLK for k in range(K)]
+            at = [lidx_ref[k, r] // BLK for k in range(K)]
             lefts = []
             for o in range(3):
                 c = [(at[k] == o).astype(F32) for k in range(K)]
@@ -433,29 +524,12 @@
     started += terms
 
     take(second)
-    inverse2 = inverse_factor(sum_grp(1) / total_rows)
-    wide2 = wide(inverse2)
-
-    def finish(q, carry):
-        basis_ref[:, columns(q)] = times(wide2, halves[:, columns(q)])
-        return carry
-
-    lax.fori_loop(0, PAIRS, finish, 0, unroll=4)
-
+    inverse_ref[...] = inverse_factor(sum_grp(1) / total_rows)
     take(terms)
     acc = final[0]
     for i in range(1, members):
         acc = acc + final[i]
-    square = inverse2[:, :TS]
-    for o in range(3):
-        packed = acc[o * HALF : (o + 1) * HALF]
-        h = jnp.concatenate([packed[:, :TS], roll(packed)[:, :TS]], axis=0)
-        left = lax.dot_general(square, h, NN, precision=lax.Precision.HIGHEST, preferred_element_type=F32)
-        full = lax.dot_general(left, square, NT, precision=lax.Precision.HIGHEST, preferred_element_type=F32)
-        tail[:, o * LANES : o * LANES + TS] = full * (groups / total_rows)
-    mine = pl.ds(pl.multiple_of(s * 8, 8), 8)
-    for o in range(3):
-        coarse_ref[:, o * TS : (o + 1) * TS] = tail[mine, o * LANES : o * LANES + TS]
+    acc_ref[...] = acc
     for c in started:
         c.wait_send()
     for c in [bulk(info_got, info_send, info_recv)] + [
@@ -464,20 +538,26 @@
         c.wait_send()
 
 
-def whole(index, lidx, info, shift2, start, x, groups, members, total_rows):
-    vmem, smem = pl.BlockSpec(memory_space=pltpu.VMEM), pl.BlockSpec(memory_space=pltpu.SMEM)
+def whole(owner, slot, nbr, shift, start, x, groups, members, total_rows):
+    vmem = pl.BlockSpec(memory_space=pltpu.VMEM)
     dma = pltpu.SemaphoreType.DMA
     count = groups * members
     tiles = x.shape[2]
     return pl.pallas_call(
         functools.partial(whole_kernel, groups, members, total_rows),
         out_shape=(
-            jax.ShapeDtypeStruct((TS, ROWS), F32),
-            jax.ShapeDtypeStruct((TS // members, 3 * TS), F32),
+            jax.ShapeDtypeStruct((2 * TS, ROWS), BF16),
+            jax.ShapeDtypeStruct((TS, LANES), F32),
+            jax.ShapeDtypeStruct((3 * HALF, LANES), F32),
         ),
-        in_specs=[smem, smem, vmem, vmem, vmem, pl.BlockSpec(memory_space=pl.ANY)],
-        out_specs=(vmem, vmem),
+        in_specs=[vmem, vmem, vmem, vmem, vmem, pl.BlockSpec(memory_space=pl.ANY)],
+        out_specs=(vmem, vmem, vmem),
         scratch_shapes=[
+            pltpu.VMEM((1, CAP * count), jnp.int32),
+            pltpu.SMEM((1, CAP * count), jnp.int32),
+            pltpu.VMEM((8, LANES), jnp.int32),
+            pltpu.SMEM((8, LANES), jnp.int32),
+            pltpu.VMEM((count, 1, LANES), F32),
             pltpu.VMEM((2, HALF * TS, tiles), F32),
             pltpu.VMEM((tiles, HALF, LANES), F32),
             pltpu.VMEM((CAP, count, HALF, LANES), F32),
@@ -491,21 +571,20 @@
             pltpu.VMEM((2, TS, ROWS), F32),
             pltpu.VMEM((2, TS, ROWS), F32),
             pltpu.VMEM((TS, ROWS), F32),
-            pltpu.VMEM((2 * TS, ROWS), BF16),
             pltpu.VMEM((3, 2 * TS, ROWS), BF16),
             pltpu.VMEM((2, members, HALF, LANES), F32),
             pltpu.VMEM((2, groups, HALF, LANES), F32),
             pltpu.VMEM((4, HALF, LANES), F32),
             pltpu.VMEM((members, 3 * HALF, LANES), F32),
             pltpu.VMEM((3 * HALF, LANES), F32),
-            pltpu.VMEM((TS, 3 * LANES), F32),
+            dma((2,)),
             dma((2,)),
             dma((CAP,)),
             dma((CAP,)),
             dma,
             dma,
-            dma((3, 2)),
-            dma((3, 2)),
+            dma((3, 2, PIECES)),
+            dma((3, 2, PIECES)),
             dma((2, members - 1)),
             dma((2, members - 1)),
             dma((2, groups - 1)),
@@ -516,35 +595,65 @@
         compiler_params=pltpu.CompilerParams(
             collective_id=1, has_side_effects=True, vmem_limit_bytes=60 << 20
         ),
-    )(index, lidx, info, shift2, start, x)
+    )(owner, slot, nbr, shift, start, x)
+
+
+def finish_kernel(groups, members, total_rows, halves_ref, inverse_ref, acc_ref, basis_ref, coarse_ref, tail):
+    inverse = inverse_ref[...]
+    step = pl.program_id(0)
+    basis_ref[...] = times(wide(inverse), halves_ref[...])
+
+    @pl.when(step == 0)
+    def _():
+        square = inverse[:, :TS]
+        for o in range(3):
+            packed = acc_ref[o * HALF : (o + 1) * HALF]
+            h = jnp.concatenate([packed[:, :TS], roll(packed)[:, :TS]], axis=0)
+            left = lax.dot_general(
+                square, h, NN, precision=lax.Precision.HIGHEST, preferred_element_type=F32
+            )
+            full = lax.dot_general(
+                left, square, NT, precision=lax.Precision.HIGHEST, preferred_element_type=F32
+            )
+            tail[:, o * LANES : o * LANES + TS] = full * (groups / total_rows)
+        each = TS // members
+        mine = pl.ds(pl.multiple_of(lax.axis_index("sub") * each, each), each)
+        for o in range(3):
+            coarse_ref[:, o * TS : (o + 1) * TS] = tail[mine, o * LANES : o * LANES + TS]
+
+
+def finish(halves, inverse, acc, groups, members, total_rows):
+    steps = 4
+    return pl.pallas_call(
+        functools.partial(finish_kernel, groups, members, total_rows),
+        out_shape=(
+            jax.ShapeDtypeStruct((TS, ROWS), F32),
+            jax.ShapeDtypeStruct((TS // members, 3 * TS), F32),
+        ),
+        grid=(steps,),
+        in_specs=[
+            pl.BlockSpec((2 * TS, ROWS // steps), lambda i: (0, i)),
+            pl.BlockSpec((TS, LANES), lambda i: (0, 0)),
+            pl.BlockSpec((3 * HALF, LANES), lambda i: (0, 0)),
+        ],
+        out_specs=(
+            pl.BlockSpec((TS, ROWS // steps), lambda i: (0, i)),
+            pl.BlockSpec((TS // members, 3 * TS), lambda i: (0, 0)),
+        ),
+        scratch_shapes=[pltpu.VMEM((TS, 3 * LANES), F32)],
+    )(halves, inverse, acc)
 
 
 def shards(tiles, owner, slot, nbr, shift, start):
-    axes = ("grp", "sub")
     groups, members = lax.axis_size("grp"), lax.axis_size("sub")
-    devices = groups * members
-    me = lax.axis_index(axes)
+    total_rows = float(ROWS * groups * members)
     count = tiles.shape[0]
-    total_blocks = BLK * devices
-    dest = owner[:, 0]
-
-    order = jnp.arange(count, dtype=jnp.int32)
-    earlier = (dest[:, None] == dest[None, :]) & (order[:, None] < order[None, :])
-    rank = jnp.sum(earlier.astype(jnp.int32), axis=0)
-    place = dest * CAP + rank
-    hit = place[:, None] == jnp.arange(devices * CAP, dtype=jnp.int32)[None, :]
-    index = jnp.sum(jnp.where(hit, order[:, None], 0), axis=0)
-    named = jnp.sum(jnp.where(hit, slot[:, None] - SLOTS, 0), axis=0) + SLOTS
-    info = jnp.pad(
-        named.astype(F32).reshape(devices, 1, CAP),
-        ((0, 0), (0, 0), (0, LANES - CAP)),
+    x = tiles.transpose(1, 2, 0).reshape(2, HALF * TS, count)
+    halves, inverse, acc = whole(
+        owner.T, slot.reshape(1, count), nbr.T, shift.reshape(PAIRS, LANES), start.T, x,
+        groups, members, total_rows,
     )
-    x = tiles.transpose(1, 2, 0).reshape(2, HALF * TS, count)
-    lidx = ((nbr - (me - 1) * BLK) % total_blocks).reshape(SLOTS)
-    twice = jnp.tile(shift.reshape(BLK, TS), (1, 2))
-    basis, coarse = whole(
-        index, lidx, info, twice, start.T, x, groups, members, float(total_blocks * TS)
-    )
+    basis, coarse = finish(halves, inverse, acc, groups, members, total_rows)
     return basis.T, coarse[None]
 
 

time: 199 us -> 175 us (0.88)
  Pallas kernels: 188 us -> 174 us
  local copies, waits for them, and re-layouts: 6.19 us -> 0 us
  other arithmetic: 3.68 us -> 0 us
    pallas_call x1, Pallas kernels: 188 us -> 170 us  [whole(): pl.pallas_call(functools.partial(whole_kernel, groups, members, total_row...]
    pallas_call x0 -> x1, Pallas kernels: none -> 4.39 us  [finish(): pl.pallas_call(functools.partial(finish_kernel, groups, members, total_ro...]
    unnamed x2 -> x0, local copies, waits for them, and re-layouts: 3.17 us -> none
where the time goes in v3:
time: 175 us
  Pallas kernels  174 us (99%)
    pallas_call x1, Pallas kernels, whole(): pl.pallas_call(functools.partial(whole_kernel, groups, members, total_row...  170 us
    pallas_call x1, Pallas kernels, finish(): pl.pallas_call(functools.partial(finish_kernel, groups, members, total_ro...  4.39 us

profile of v3, /device:TPU:1, one launch (start us, length us, event | category | flops | bytes accessed | tf_op | source)
XLA Modules:
  0.0 174.7 jit_solution(15118806280294028664)
XLA Ops:
  0.6 169.7 %shard_map.77 = (bf16[128,2048]{1,0:T(8,128)(2,1)}, f32[64,128]{1,0:T(8,128)}, f32[96,128]{1,0:T(8,128)}) custom-call(s32[1,256]{1,0:T(1,128)} %bitcast.14, s32[1,256]{1,0:T(1,128)} %bitcast.15, s32[5,32]{1,0:T(8,128)} %bitcast.13, f32[16,128]{1,0:T(8,128)} %bitcast.12, f32[64,2048]{1,0:T(8,128)} %bitcast.11, f32[2,2048,256]{2,1,0:T(8,128)} %bitcast.10), custom_call_target="tpu_custom_call" | custom-call | tf_op jit(solution)/shard_map/pallas_call | solution.py:546
  170.3 4.4 %shard_map.78 = (f32[64,2048]{1,0:T(8,128)}, f32[8,192]{1,0:T(8,128)}) custom-call(bf16[128,2048]{1,0:T(8,128)(2,1)} %get-tuple-element.7.halves_ref, f32[64,128]{1,0:T(8,128)} %get-tuple-element.8.inverse_ref, f32[96,128]{1,0:T(8,128)} %get-tuple-element.9.acc_ref), custom_call_target="tpu_custom_call" | custom-call | tf_op jit(solution)/shard_map/pallas_call | solution.py:627

commit v4 on v3

--- a/solution.py
+++ b/solution.py
@@ -11,11 +11,13 @@
 CAP = 4
 TS = 64
 HALF = 32
+PITCH = 40
 LANES = 128
 BLK = 32
 ROWS = BLK * TS
 PAIRS = ROWS // LANES
 SLOTS = BLK * K
+DEPTH = SLOTS + 8
 NT = (((1,), (1,)), ((), ()))
 NN = (((1,), (0,)), ((), ()))
 PIECES = 4
@@ -30,6 +32,10 @@
     return lax.dot_general(a, b, dims, preferred_element_type=F32)
 
 
+def exact(a, b, dims):
+    return lax.dot_general(a, b, dims, precision=lax.Precision.HIGHEST, preferred_element_type=F32)
+
+
 def roll(x):
     return pltpu.roll(x, TS, axis=1)
 
@@ -46,6 +52,20 @@
 
 def fold(out):
     t = out[:TS] + out[TS:]
+    return t + roll(t)
+
+
+def gram_parts(x):
+    hi = x.astype(BF16)
+    rest = x - hi.astype(F32)
+    mid = rest.astype(BF16)
+    lo = (rest - mid.astype(F32)).astype(BF16)
+    return jnp.concatenate([hi, mid, lo, jnp.zeros_like(lo)], axis=0)
+
+
+def fold_gram(out):
+    t = out[:TS] + out[TS : 2 * TS] + out[2 * TS : 3 * TS]
+    t = t[:, :LANES] + t[:, LANES:]
     return t + roll(t)
 
 
@@ -222,7 +242,7 @@
             packed[pl.ds(h * LANES, LANES), c, :] = block.T
 
     def tile(position):
-        return packed[jnp.clip(index_ref[0, position], 0, amount - 1)]
+        return packed[jnp.clip(index_ref[0, position], 0, amount - 1)][:HALF]
 
     for c in tables:
         c.wait()
@@ -303,10 +323,12 @@
         info_copy(i).start()
         return carry
 
+    landing = pl.ds(pl.multiple_of(me * PITCH, 8), HALF)
+
     def send_tile(k, i):
         other, place = peer_of(i)
         sent[k, other] = tile(k * count + other)
-        remote(sent.at[k, other], got.at[k, me], tile_send.at[k], tile_recv.at[k], place).start()
+        remote(sent.at[k, other], got.at[k, landing], tile_send.at[k], tile_recv.at[k], place).start()
 
     def send_tiles(k):
         def send(i, carry):
@@ -320,10 +342,11 @@
         return remote(part, part, send, recv, device(after))
 
     def arrived(k):
-        bulk(got.at[k], tile_send.at[k], tile_recv.at[k]).wait_recv()
+        part = got.at[k, pl.ds(0, (count - 1) * HALF)]
+        remote(part, part, tile_send.at[k], tile_recv.at[k], device(after)).wait_recv()
 
     for k in range(CAP):
-        got[k, me] = tile(k * count + me)
+        got[k, landing] = tile(k * count + me)
     info_got[me] = info_ref[me]
     send_tiles(0)
     lax.fori_loop(0, count - 1, send_info, 0)
@@ -344,8 +367,9 @@
         return jnp.concatenate([hot, hot], axis=1)
 
     def add(k, hot, c):
-        new = dot(hot, split(got[k, :, c, :]), NN)
-        total[c] = new if k == 0 else total[c] + new
+        new = dot(hot, split(got[k, pl.ds(c, count, stride=PITCH), :]), NN)
+        at = pl.ds(pl.multiple_of(c * DEPTH, 8), SLOTS)
+        total[at] = new if k == 0 else total[at] + new
 
     for k in range(2, CAP):
         arrived(k - 2)
@@ -387,7 +411,7 @@
         shift_of = [jnp.where(low[:1], both, roll(both)), jnp.where(low[:1], roll(both), both)]
         for b in range(2):
             r = 2 * q + b
-            t = [total[:, r * K + k, :] for k in range(K)]
+            t = [total[pl.ds(r * K + k, HALF, stride=DEPTH), :] for k in range(K)]
             t[0] = t[0] + jnp.where(on_diagonal, shift_of[b], 0.0)
             for j in range(3):
                 x = t[2 * j]
@@ -422,54 +446,61 @@
         return carry
 
     def products(out, halo, n):
-        copies = []
+        copies, gram = [], None
         for p in range(PIECES):
             lax.fori_loop(
                 p * (PAIRS // PIECES), (p + 1) * (PAIRS // PIECES),
                 functools.partial(product, out), 0, unroll=4,
             )
             copies.append(send_halo(out, halo, n, p))
-        return copies
-
-    halo = products(x1, halo1, 1)
+            parts = gram_parts(out[:, piece(p)])
+            part = dot(parts, parts, NT)
+            gram = part if gram is None else gram + part
+        return copies, pack(fold_gram(gram))
+
+    halo, partial[0] = products(x1, halo1, 1)
     started += sum(halo, [])
 
+    first = send_grp(partial.at[0], 0)
+    grp_got[0, g] = partial[0]
+
     def own1(q, carry):
-        x = x1[:, columns(q)]
+        put_pair(BLK, q, x1[:, columns(q)])
+        return carry
+
+    lax.fori_loop(0, PAIRS, own1, 0, unroll=4)
+    spread_halos(halo1, halo)
+    take(first)
+    partial[1] = sum_grp(0)
+    second = send_sub(partial.at[1], sub_got, sub_send, sub_recv, 0)
+    sub_got[0, s] = partial[1]
+    started += first + second
+
+    halo, partial[2] = products(z, halo2, 2)
+    started += sum(halo, [])
+    third = send_grp(partial.at[2], 1)
+    grp_got[1, g] = partial[2]
+
+    take(second)
+    inverse1 = inverse_factor(sum_sub(0) / total_rows)
+    wide1 = wide(inverse1)
+
+    take(third)
+    partial[3] = sum_grp(1)
+    fourth = send_sub(partial.at[3], sub_got, sub_send, sub_recv, 1)
+    sub_got[1, s] = partial[3]
+    started += third + fourth
+
+    def own2(q, carry):
+        x = times(wide1, split(z[:, columns(q)]))
         halves[:, columns(q)] = split(x)
         put_pair(BLK, q, x)
         return carry
 
-    lax.fori_loop(0, PAIRS, own1, 0, unroll=2)
-    partial[3] = pack(fold(dot(halves[...], halves[...], NT)))
-
-    first = send_sub(partial.at[3], sub_got, sub_send, sub_recv, 0)
-    sub_got[0, s] = partial[3]
-    take(first)
-    partial[0] = sum_sub(0)
-    grp_got[0, g] = partial[0]
-    second = send_grp(partial.at[0], 0)
-    started += first + second
-    spread_halos(halo1, halo)
-    halo = products(z, halo2, 2)
-    started += sum(halo, [])
-
-    take(second)
-    inverse1 = wide(inverse_factor(sum_grp(0) / total_rows))
-
-    def own2(q, carry):
-        x = times(inverse1, split(z[:, columns(q)]))
-        halves[:, columns(q)] = split(x)
-        put_pair(BLK, q, x)
-        return carry
-
     lax.fori_loop(0, PAIRS, own2, 0, unroll=4)
-    partial[1] = pack(fold(dot(halves[...], halves[...], NT)))
-    first = send_sub(partial.at[1], sub_got, sub_send, sub_recv, 1)
-    sub_got[1, s] = partial[1]
 
     def ext2(side, q, carry):
-        put_pair(side * 2 * BLK, q, times(inverse1, split(halo2[side, :, columns(q)])))
+        put_pair(side * 2 * BLK, q, times(wide1, split(halo2[side, :, columns(q)])))
         return carry
 
     for p in range(PIECES):
@@ -479,12 +510,6 @@
                 p * (PAIRS // PIECES), (p + 1) * (PAIRS // PIECES),
                 functools.partial(ext2, side), 0, unroll=4,
             )
-
-    take(first)
-    partial[2] = sum_sub(1)
-    grp_got[1, g] = partial[2]
-    second = send_grp(partial.at[2], 1)
-    started += first + second
 
     low, high = masks
 
@@ -507,7 +532,7 @@
             mapped[o, :, columns(q)] = split(x)
         return carry
 
-    lax.fori_loop(0, PAIRS, project, 0, unroll=2)
+    lax.fori_loop(0, PAIRS, project, 0, unroll=4)
     h = [fold(dot(halves[...], mapped[o], NT)) for o in range(3)]
     is_first = (s == 0).astype(F32)
     is_last = (s == members - 1).astype(F32)
@@ -523,8 +548,12 @@
     final[s] = term[...]
     started += terms
 
-    take(second)
-    inverse_ref[...] = inverse_factor(sum_grp(1) / total_rows)
+    take(fourth)
+    packed_gram = sum_sub(1) / total_rows
+    square = inverse1[:, :TS]
+    gram = jnp.concatenate([packed_gram[:, :TS], roll(packed_gram)[:, :TS]], axis=0)
+    gram = exact(exact(square, gram, NN), square, NT)
+    inverse_ref[...] = inverse_factor(jnp.concatenate([gram[:HALF], gram[HALF:]], axis=1))
     take(terms)
     acc = final[0]
     for i in range(1, members):
@@ -559,11 +588,11 @@
             pltpu.SMEM((8, LANES), jnp.int32),
             pltpu.VMEM((count, 1, LANES), F32),
             pltpu.VMEM((2, HALF * TS, tiles), F32),
-            pltpu.VMEM((tiles, HALF, LANES), F32),
+            pltpu.VMEM((tiles, PITCH, LANES), F32),
             pltpu.VMEM((CAP, count, HALF, LANES), F32),
-            pltpu.VMEM((CAP, count, HALF, LANES), F32),
+            pltpu.VMEM((CAP, count * PITCH, LANES), F32),
             pltpu.VMEM((count, 1, LANES), F32),
-            pltpu.VMEM((HALF, SLOTS, LANES), F32),
+            pltpu.VMEM((HALF * DEPTH, LANES), F32),
             pltpu.VMEM((BLK, 2 * TS, 3 * LANES), BF16),
             pltpu.VMEM((TS, ROWS), F32),
             pltpu.VMEM((3 * BLK, 2 * TS, LANES), BF16),
@@ -606,16 +635,15 @@
     @pl.when(step == 0)
     def _():
         square = inverse[:, :TS]
+        sides = []
         for o in range(3):
             packed = acc_ref[o * HALF : (o + 1) * HALF]
-            h = jnp.concatenate([packed[:, :TS], roll(packed)[:, :TS]], axis=0)
-            left = lax.dot_general(
-                square, h, NN, precision=lax.Precision.HIGHEST, preferred_element_type=F32
-            )
-            full = lax.dot_general(
-                left, square, NT, precision=lax.Precision.HIGHEST, preferred_element_type=F32
-            )
-            tail[:, o * LANES : o * LANES + TS] = full * (groups / total_rows)
+            sides.append(jnp.concatenate([packed, roll(packed)], axis=0))
+        left = exact(square, jnp.concatenate(sides, axis=1), NN)
+        left = jnp.concatenate([left[:, o * LANES : o * LANES + TS] for o in range(3)], axis=0)
+        full = exact(left, square, NT) * (groups / total_rows)
+        for o in range(3):
+            tail[:, o * LANES : o * LANES + TS] = full[o * TS : (o + 1) * TS]
         each = TS // members
         mine = pl.ds(pl.multiple_of(lax.axis_index("sub") * each, each), each)
         for o in range(3):
@@ -623,7 +651,7 @@
 
 
 def finish(halves, inverse, acc, groups, members, total_rows):
-    steps = 4
+    steps = 2
     return pl.pallas_call(
         functools.partial(finish_kernel, groups, members, total_rows),
         out_shape=(

time: 175 us -> 156 us (0.89)
  Pallas kernels: 174 us -> 156 us
    pallas_call x1, Pallas kernels: 170 us -> 153 us  [whole(): pl.pallas_call(functools.partial(whole_kernel, groups, members, total_row...]
where the time goes in v4:
time: 156 us
  Pallas kernels  156 us (100%)
    pallas_call x1, Pallas kernels, whole(): pl.pallas_call(functools.partial(whole_kernel, groups, members, total_row...  153 us

profile of v4, /device:TPU:1, one launch (start us, length us, event | category | flops | bytes accessed | tf_op | source)
XLA Modules:
  0.0 156.2 jit_solution(12225345453442040271)
XLA Ops:
  0.6 152.9 %shard_map.77 = (bf16[128,2048]{1,0:T(8,128)(2,1)}, f32[64,128]{1,0:T(8,128)}, f32[96,128]{1,0:T(8,128)}) custom-call(s32[1,256]{1,0:T(1,128)} %bitcast.14, s32[1,256]{1,0:T(1,128)} %bitcast.15, s32[5,32]{1,0:T(8,128)} %bitcast.13, f32[16,128]{1,0:T(8,128)} %bitcast.12, f32[64,2048]{1,0:T(8,128)} %bitcast.11, f32[2,2048,256]{2,1,0:T(8,128)} %bitcast.10), custom_call_target="tpu_custom_call" | custom-call | tf_op jit(solution)/shard_map/pallas_call | solution.py:575
  153.5 2.7 %shard_map.78 = (f32[64,2048]{1,0:T(8,128)}, f32[8,192]{1,0:T(8,128)}) custom-call(bf16[128,2048]{1,0:T(8,128)(2,1)} %get-tuple-element.7.halves_ref, f32[64,128]{1,0:T(8,128)} %get-tuple-element.8.inverse_ref, f32[96,128]{1,0:T(8,128)} %get-tuple-element.9.acc_ref), custom_call_target="tpu_custom_call" | custom-call | tf_op jit(solution)/shard_map/pallas_call | solution.py:655

commit v5 on v4

--- a/solution.py
+++ b/solution.py
@@ -21,8 +21,8 @@
 NT = (((1,), (1,)), ((), ()))
 NN = (((1,), (0,)), ((), ()))
 PIECES = 4
-STRIDE = 37
-SHIFT = 51
+STRIDE = 53
+SHIFT = 76
 MESH = pl.DeviceIdType.MESH
 F32 = jnp.float32
 BF16 = jnp.bfloat16

time: 156 us -> 156 us (level)
  no operation moved by 1% of the time
where the time goes in v5:
time: 156 us
  Pallas kernels  156 us (100%)
    pallas_call x1, Pallas kernels, whole(): pl.pallas_call(functools.partial(whole_kernel, groups, members, total_row...  153 us

profile of v5, /device:TPU:1, one launch (start us, length us, event | category | flops | bytes accessed | tf_op | source)
XLA Modules:
  0.0 156.3 jit_solution(14600619764486689775)
XLA Ops:
  0.6 153.0 %shard_map.77 = (bf16[128,2048]{1,0:T(8,128)(2,1)}, f32[64,128]{1,0:T(8,128)}, f32[96,128]{1,0:T(8,128)}) custom-call(s32[1,256]{1,0:T(1,128)} %bitcast.14, s32[1,256]{1,0:T(1,128)} %bitcast.15, s32[5,32]{1,0:T(8,128)} %bitcast.13, f32[16,128]{1,0:T(8,128)} %bitcast.12, f32[64,2048]{1,0:T(8,128)} %bitcast.11, f32[2,2048,256]{2,1,0:T(8,128)} %bitcast.10), custom_call_target="tpu_custom_call" | custom-call | tf_op jit(solution)/shard_map/pallas_call | solution.py:575
  153.6 2.7 %shard_map.78 = (f32[64,2048]{1,0:T(8,128)}, f32[8,192]{1,0:T(8,128)}) custom-call(bf16[128,2048]{1,0:T(8,128)(2,1)} %get-tuple-element.7.halves_ref, f32[64,128]{1,0:T(8,128)} %get-tuple-element.8.inverse_ref, f32[96,128]{1,0:T(8,128)} %get-tuple-element.9.acc_ref), custom_call_target="tpu_custom_call" | custom-call | tf_op jit(solution)/shard_map/pallas_call | solution.py:655

commit v6 on v5

--- a/solution.py
+++ b/solution.py
@@ -590,9 +590,9 @@
             pltpu.VMEM((2, HALF * TS, tiles), F32),
             pltpu.VMEM((tiles, PITCH, LANES), F32),
             pltpu.VMEM((CAP, count, HALF, LANES), F32),
-            pltpu.VMEM((CAP, count * PITCH, LANES), F32),
+            pltpu.VMEM((CAP, (count + 1) * PITCH, LANES), F32),
             pltpu.VMEM((count, 1, LANES), F32),
-            pltpu.VMEM((HALF * DEPTH, LANES), F32),
+            pltpu.VMEM(((HALF + 1) * DEPTH, LANES), F32),
             pltpu.VMEM((BLK, 2 * TS, 3 * LANES), BF16),
             pltpu.VMEM((TS, ROWS), F32),
             pltpu.VMEM((3 * BLK, 2 * TS, LANES), BF16),

time: 156 us -> 156 us (level)
  no operation moved by 1% of the time
where the time goes in v6:
time: 156 us
  Pallas kernels  156 us (100%)
    pallas_call x1, Pallas kernels, whole(): pl.pallas_call(functools.partial(whole_kernel, groups, members, total_row...  153 us

profile of v6, /device:TPU:1, one launch (start us, length us, event | category | flops | bytes accessed | tf_op | source)
XLA Modules:
  0.0 156.3 jit_solution(12885793107751108106)
XLA Ops:
  0.6 153.0 %shard_map.77 = (bf16[128,2048]{1,0:T(8,128)(2,1)}, f32[64,128]{1,0:T(8,128)}, f32[96,128]{1,0:T(8,128)}) custom-call(s32[1,256]{1,0:T(1,128)} %bitcast.14, s32[1,256]{1,0:T(1,128)} %bitcast.15, s32[5,32]{1,0:T(8,128)} %bitcast.13, f32[16,128]{1,0:T(8,128)} %bitcast.12, f32[64,2048]{1,0:T(8,128)} %bitcast.11, f32[2,2048,256]{2,1,0:T(8,128)} %bitcast.10), custom_call_target="tpu_custom_call" | custom-call | tf_op jit(solution)/shard_map/pallas_call | solution.py:575
  153.6 2.7 %shard_map.78 = (f32[64,2048]{1,0:T(8,128)}, f32[8,192]{1,0:T(8,128)}) custom-call(bf16[128,2048]{1,0:T(8,128)(2,1)} %get-tuple-element.7.halves_ref, f32[64,128]{1,0:T(8,128)} %get-tuple-element.8.inverse_ref, f32[96,128]{1,0:T(8,128)} %get-tuple-element.9.acc_ref), custom_call_target="tpu_custom_call" | custom-call | tf_op jit(solution)/shard_map/pallas_call | solution.py:655
